TPU v7x, 256 devices: a whole 4x4x8 slice. The times are simulated.
256 devices in a mesh: dp: 4 (over x), expert: 16 (over z, core), etp: 4 (over y).
Axes of the slice: x: 4, y: 4, z: 8, core: 2. Of those that a mesh axis runs over, the one named last changes fastest.
Arguments:
- tokens: bfloat16 [2048, 3072], P(('dp', 'expert')), may hold values from -6 to 6
- out_grad: bfloat16 [2048, 3072], P(('dp', 'expert')), may hold values from -6 to 6
- gates: bfloat16 [2048, 4], P(('dp', 'expert')), may hold values from 0.099609375 to 1
- expert_ids: int32 [2048, 4], P(('dp', 'expert')), may hold values from 0 to 15, all different within a row; in each aligned block of 32 rows (0 to 31, 32 to 63, ...) at most 12 rows name the same one
- w_gate: bfloat16 [16, 5376, 3072], P('expert', ('dp', 'etp')), may hold values from -0.109375 to 0.109375
- w_up: bfloat16 [16, 5376, 3072], P('expert', ('dp', 'etp')), may hold values from -0.109375 to 0.109375
- w_down: bfloat16 [16, 5376, 3072], P('expert', ('dp', 'etp')), may hold values from -0.078125 to 0.078125
Outputs:
- input_grad: bfloat16 [2048, 3072], P(('dp', 'expert'), 'etp')
- gate_grad: float32 [2048, 4], P(('dp', 'expert', 'etp'))
- grad_gate: bfloat16 [16, 5376, 3072], P('expert', ('dp', 'etp'))
- grad_up: bfloat16 [16, 5376, 3072], P('expert', ('dp', 'etp'))
- grad_down: bfloat16 [16, 5376, 3072], P('expert', ('dp', 'etp'))
Inputs may be any that keep to these rules, and one draw needn't show every extreme that they name: `expert_ids`: in each aligned block of 32 rows (the tokens of one device along dp and expert) no expert is named by more than 12 rows, a bound that some block reaches. A row names 4 different experts.
All inputs are finite; a program needn't handle non-finite values.
Results may differ from a plain program's by a relative error of at most 0.0049.
Values may be sent and summed in bfloat16 or wider, within the bound.
A program may use at most 128 MiB of HBM per device.

v0:
```python
import jax
import jax.numpy as jnp
from jax import lax
from jax.sharding import PartitionSpec as P

EXPERTS = 16
TOP = 4
CAP = 12


highest = lax.Precision.HIGHEST


def slot_tables(routes):
    blocks, count, choose = routes.shape
    flat = routes.reshape(blocks, count * choose)
    labels = jnp.arange(EXPERTS, dtype=jnp.int32)
    onehot = (flat[:, :, None] == labels).astype(jnp.int32)
    earlier = jnp.cumsum(onehot, axis=1) - onehot
    position = jnp.sum(earlier * onehot, axis=2)
    places = jnp.arange(CAP, dtype=jnp.int32)
    hits = onehot[:, :, :, None] * (position[:, :, None, None] == places).astype(jnp.int32)
    return hits.astype(jnp.float32).reshape(blocks, count, choose, EXPERTS, CAP)


def per_device(tokens, out_grad, gates, expert_ids, w_gate, w_up, w_down):
    groups = lax.axis_size("dp")
    spread = lax.axis_size("expert")
    etp_size = lax.axis_size("etp")
    local_experts, hidden, model_width = w_gate.shape
    tok_dev = tokens.shape[0]
    slice_width = model_width // etp_size
    row_count = groups * spread * CAP
    own_hits = slot_tables(expert_ids[None])[0].reshape(tok_dev, TOP, spread, local_experts, CAP)
    own_table = jnp.sum(own_hits, axis=1)
    table_half = own_table.astype(jnp.bfloat16)
    row_buffer = jnp.einsum(
        "tnxc,td->xncd", table_half, tokens, preferred_element_type=jnp.float32
    ).astype(jnp.bfloat16)
    grad_buffer = jnp.einsum(
        "tnxc,td->xncd", table_half, out_grad, preferred_element_type=jnp.float32
    ).astype(jnp.bfloat16)
    gate_buffer = jnp.einsum(
        "tknxc,tk->xnc", own_hits, gates.astype(jnp.float32), precision=highest
    ).astype(jnp.bfloat16)
    row_buffer, grad_buffer, gate_buffer = (
        lax.all_to_all(row_buffer, "expert", split_axis=1, concat_axis=1, tiled=True),
        lax.all_to_all(grad_buffer, "expert", split_axis=1, concat_axis=1, tiled=True),
        lax.all_to_all(gate_buffer, "expert", split_axis=1, concat_axis=1, tiled=True),
    )
    gathered = (
        lax.all_gather(
            row_buffer.reshape(local_experts, 1, spread * CAP, model_width),
            "dp",
            axis=1,
            tiled=True,
        ),
        lax.all_gather(
            grad_buffer.reshape(local_experts, 1, spread * CAP, model_width),
            "dp",
            axis=1,
            tiled=True,
        ),
        lax.all_gather(
            gate_buffer.reshape(local_experts, 1, spread * CAP), "dp", axis=1, tiled=True
        ),
    )
    expert_rows = gathered[0].reshape(local_experts, row_count, model_width)
    grad_rows = gathered[1].reshape(local_experts, row_count, model_width)
    scales = gathered[2].reshape(local_experts, 1, row_count).astype(jnp.float32)
    pre_gate = jnp.einsum("xfd,xrd->xfr", w_gate, expert_rows, preferred_element_type=jnp.float32)
    pre_up = jnp.einsum("xfd,xrd->xfr", w_up, expert_rows, preferred_element_type=jnp.float32)
    raw_grad = jnp.einsum("xfd,xrd->xfr", w_down, grad_rows, preferred_element_type=jnp.float32)
    sigmoid_gate = jax.nn.sigmoid(pre_gate)
    activated = pre_gate * sigmoid_gate
    product = activated * pre_up
    gate_terms = (
        jnp.sum(product * raw_grad, axis=1)
        .reshape(local_experts, groups, spread, CAP)
        .transpose(1, 0, 2, 3)
    )
    scaled = (scales * product).astype(jnp.bfloat16)
    grad_down = jnp.einsum(
        "xfr,xrd->xfd", scaled, grad_rows, preferred_element_type=jnp.float32
    ).astype(jnp.bfloat16)
    hidden_grad = scales * raw_grad
    grad_pre_gate = (
        hidden_grad * pre_up * sigmoid_gate * (1.0 + pre_gate * (1.0 - sigmoid_gate))
    ).astype(jnp.bfloat16)
    grad_pre_up = (hidden_grad * activated).astype(jnp.bfloat16)
    grad_gate = jnp.einsum(
        "xfr,xrd->xfd", grad_pre_gate, expert_rows, preferred_element_type=jnp.float32
    ).astype(jnp.bfloat16)
    grad_up = jnp.einsum(
        "xfr,xrd->xfd", grad_pre_up, expert_rows, preferred_element_type=jnp.float32
    ).astype(jnp.bfloat16)
    partial_value = jnp.einsum(
        "xfpsk,xfcd->pcxskd",
        grad_pre_gate.reshape(local_experts, hidden, groups, spread, CAP),
        w_gate.reshape(local_experts, hidden, etp_size, slice_width),
        preferred_element_type=jnp.float32,
    )
    partial_value = partial_value + jnp.einsum(
        "xfpsk,xfcd->pcxskd",
        grad_pre_up.reshape(local_experts, hidden, groups, spread, CAP),
        w_up.reshape(local_experts, hidden, etp_size, slice_width),
        preferred_element_type=jnp.float32,
    )
    spread_terms = jnp.broadcast_to(
        gate_terms[:, None], (groups, etp_size, local_experts, spread, CAP)
    ).reshape(groups * etp_size, local_experts, spread, CAP)
    summed, summed_terms = (
        lax.psum_scatter(
            partial_value.reshape(groups * etp_size, local_experts, spread, CAP, slice_width),
            ("dp", "etp"),
            scatter_dimension=0,
            tiled=True,
        ),
        lax.psum_scatter(spread_terms, ("dp", "etp"), scatter_dimension=0, tiled=True),
    )
    returned, returned_terms = (
        lax.all_to_all(summed[0], "expert", split_axis=1, concat_axis=1, tiled=True),
        lax.all_to_all(summed_terms[0], "expert", split_axis=1, concat_axis=1, tiled=True),
    )
    input_grad = jnp.einsum("tnxc,xncd->td", own_table, returned, precision=highest)
    gate_grad = jnp.einsum("tknxc,xnc->tk", own_hits, returned_terms, precision=highest)
    share_rows = tok_dev // etp_size
    gate_grad = lax.dynamic_slice_in_dim(
        gate_grad, lax.axis_index("etp") * share_rows, share_rows, 0
    )
    return (input_grad.astype(jnp.bfloat16), gate_grad, grad_gate, grad_up, grad_down)


def solution(mesh):
    in_specs = (
        P(("dp", "expert"), None),
        P(("dp", "expert"), None),
        P(("dp", "expert"), None),
        P(("dp", "expert"), None),
        P("expert", ("dp", "etp"), None),
        P("expert", ("dp", "etp"), None),
        P("expert", ("dp", "etp"), None),
    )
    out_specs = (
        P(("dp", "expert"), "etp"),
        P(("dp", "expert", "etp"), None),
        P("expert", ("dp", "etp"), None),
        P("expert", ("dp", "etp"), None),
        P("expert", ("dp", "etp"), None),
    )
    return jax.shard_map(
        per_device, mesh=mesh, in_specs=in_specs, out_specs=out_specs, check_vma=False
    )
```

profile of v0, /device:TPU:1, one launch (start us, length us, event | category | flops | bytes accessed | tf_op | source)
XLA Modules:
  0.0 322.8 jit_solution(15465942408461652636)
XLA Ops:
  7.2 0.9 copy.87
  8.1 0.7 fusion.34
  9.6 1.4 fusion.4
  11.7 49.7 %all_to_all.25 = bf16[1,16,12,3072]{3,2,0,1:T(8,128)(2,1)} all-to-all(bf16[1,16,12,3072]{3,2,0,1:T(8,128)(2,1)S(1)} %copy.95), channel_id=1, replica_groups=mesh['dp'=4,'expert'=16,'etp'=4] {'expert'}, dimensions={1} | all-to-all | bytes 2359296 | tf_op jit(solution)/shard_map/all_to_all | solution.py:47
  61.4 2.4 reshape.313
  64.9 42.5 %all_to_all.26 = bf16[1,16,12,3072]{3,2,0,1:T(8,128)(2,1)} all-to-all(bf16[1,16,12,3072]{3,2,0,1:T(8,128)(2,1)S(1)} %copy.93), channel_id=1, replica_groups=mesh['dp'=4,'expert'=16,'etp'=4] {'expert'}, dimensions={1} | all-to-all | bytes 2359296 | tf_op jit(solution)/shard_map/all_to_all | solution.py:48
  107.5 2.3 reshape.310
  111.3 3.4 %all-to-all-start = ((bf16[1,16,12]{2,0,1:T(2,128)(2,1)}), bf16[1,16,12]{2,0,1:T(2,128)(2,1)S(1)}, u32[]{:S(2)}, u32[]{:S(2)}) async-start(bf16[1,16,12]{2,0,1:T(2,128)(2,1)} %copy.91), calls=%async_computation | async-start | bytes 16384 | tf_op jit(solution)/shard_map/all_to_all | solution.py:49
  114.7 4.8 %reshape.318 = bf16[336,4,768]{2,1,0:T(4,128)(2,1)} reshape(bf16[1,336,3072]{2,1,0:T(8,128)(2,1)} %param.11) | data formatting | bytes 4128768 | tf_op jit(solution)/shard_map/reshape.41
  119.6 4.8 %reshape.320 = bf16[336,4,768]{2,1,0:T(4,128)(2,1)} reshape(bf16[1,336,3072]{2,1,0:T(8,128)(2,1)} %param.12) | data formatting | bytes 4128768 | tf_op jit(solution)/shard_map/reshape.44
  124.6 7.9 %all_gather.9 = bf16[1,4,192]{2,0,1:T(2,128)(2,1)S(1)} all-gather(bf16[1,1,192]{2,0,1:T(2,128)(2,1)S(1)} %bitcast.115), channel_id=1, replica_groups=mesh['dp'=4,'expert'=16,'etp'=4] {'dp'}, dimensions={1}, use_global_device_ids=true | all-gather | bytes 1920 | tf_op jit(solution)/shard_map/all_gather | solution.py:64
  132.5 6.1 %fusion.20 = f32[336,768]{1,0:T(8,128)} fusion(bf16[768,3072]{1,0:T(8,128)(2,1)} %bitcast.116, bf16[1,336,3072]{2,1,0:T(8,128)(2,1)} %param.11), kind=kOutput, calls=%fused_computation.22 | convolution fusion | flops 1585446912 | bytes 7815168 | tf_op jit(solution)/shard_map/xfd,xrd->xfr/dot_general | solution.py:71
  138.7 2.8 fusion.17
  141.5 31.7 %all-gather.3.cloned.1.call-done = bf16[1,4,192,3072]{3,2,0,1:T(8,128)(2,1)} async-done(((bf16[1,1,192,3072]{3,2,0,1:T(8,128)(2,1)}), bf16[1,4,192,3072]{3,2,0,1:T(8,128)(2,1)}) %all-gather.3.cloned.1.call-update) | async-done | bytes 4718608 | tf_op jit(solution)/shard_map/all_gather | solution.py:58
  173.2 5.9 %multiply_reduce_fusion.2 = (f32[768]{0:T(1024)S(1)}, bf16[336,768]{1,0:T(8,128)(2,1)S(1)}, bf16[336,768]{1,0:T(8,128)(2,1)}) fusion(f32[336,768]{1,0:T(8,128)} %fusion.17, f32[336,768]{1,0:T(8,128)} %fusion.20, f32[768]{0:T(1024)S(1)} %reshape.324, bf16[768,3072]{1,0:T(8,128)(2,1)} %bitcast.120, bf16[1,336,3072]{2,1,0:T(8,128)(2,1)S(1)} %copy-done), kind=kOutput, calls=%fused_computation.28 | convolution fusion | flops 1589832960 | bytes 9885696 | tf_op jit(solution)/shard_map/xfd,xrd->xfr/dot_general | solution.py:73
  179.1 0.8 copy-done.10
  180.4 1.5 copy.100
  181.9 1.1 reshape.319
  182.9 2.6 fusion.6
  185.6 2.6 add_bitcast_fusion
  188.2 4.6 %copy.103 = f32[4,4,1,16,12,768]{5,3,4,2,1,0:T(8,128)} copy(f32[4,4,1,16,12,768]{5,3,1,4,0,2:T(8,128)S(1)} %add_bitcast_fusion) | data formatting | bytes 18874368 | tf_op jit(solution)/shard_map/add | solution.py:103
  194.4 61.2 %all-reduce.1 = f32[16,1,16,12]{2,1,3,0:T(1,128)S(1)} all-reduce(f32[16,1,16,12]{2,1,3,0:T(1,128)S(1)} %copy.107), channel_id=3, replica_groups=mesh['dp'=4,'expert'=16,'etp'=4] {'dp','etp'}, use_global_device_ids=true, to_apply=%region_5.6.clone | all-reduce | flops 3072 | bytes 24576
  256.2 0.7 copy.108
  256.9 21.3 %all-to-all-start.4 = ((f32[1,16,12]{2,0,1:T(1,128)}), f32[1,16,12]{2,0,1:T(1,128)S(1)}, u32[]{:S(2)}, u32[]{:S(2)}) async-start(f32[1,16,12]{2,0,1:T(1,128)} %copy.108), calls=%async_computation.4 | async-start | bytes 16384 | tf_op jit(solution)/shard_map/all_to_all | solution.py:123
  278.2 5.5 %fusion.1 = bf16[1,336,3072]{2,1,0:T(8,128)(2,1)} fusion(bf16[336,768]{1,0:T(8,128)(2,1)S(1)} %copy-done.12, bf16[768,3072]{1,0:T(8,128)(2,1)} %bitcast.117), kind=kOutput, calls=%fused_computation.5 | convolution fusion | flops 1586479104 | bytes 7299072 | tf_op jit(solution)/shard_map/xfr,xrd->xfd/dot_general | solution.py:94
  283.7 1.4 reduce-scatter.4.cloned.1.call-done
  285.1 2.5 copy.104
  287.6 8.8 %all-to-all-start.3 = ((f32[1,16,12,768]{3,0,2,1:T(1,128)}), f32[1,16,12,768]{3,0,2,1:T(1,128)S(1)}, u32[]{:S(2)}, u32[]{:S(2)}) async-start(f32[1,16,12,768]{3,0,2,1:T(1,128)} %copy.104), calls=%async_computation.3 | async-start | bytes 1179648 | tf_op jit(solution)/shard_map/all_to_all | solution.py:122
  296.4 5.6 %fusion = bf16[1,336,3072]{2,1,0:T(8,128)(2,1)} fusion(bf16[336,768]{1,0:T(8,128)(2,1)S(1)} %copy-done.11, bf16[768,3072]{1,0:T(8,128)(2,1)} %bitcast.118), kind=kOutput, calls=%fused_computation.4 | convolution fusion | flops 1586479104 | bytes 7299072 | tf_op jit(solution)/shard_map/xfr,xrd->xfd/dot_general | solution.py:91
  302.0 5.7 %fusion.2 = bf16[1,336,3072]{2,1,0:T(8,128)(2,1)} fusion(bf16[768,3072]{1,0:T(8,128)(2,1)} %bitcast.121, f32[768]{0:T(1024)S(1)} %reshape.324, f32[336,768]{1,0:T(8,128)S(1)} %copy-done.18, f32[336,768]{1,0:T(8,128)S(1)} %copy-done.17), kind=kOutput, calls=%fused_computation.6 | convolution fusion | flops 1588285440 | bytes 8850432 | tf_op jit(solution)/shard_map/xfr,xrd->xfd/dot_general | solution.py:83
  309.0 6.1 %all-to-all-done.3 = f32[1,16,12,768]{3,0,2,1:T(1,128)S(1)} async-done(((f32[1,16,12,768]{3,0,2,1:T(1,128)}), f32[1,16,12,768]{3,0,2,1:T(1,128)S(1)}, u32[]{:S(2)}, u32[]{:S(2)}) %all-to-all-start.3) | async-done | bytes 589856 | tf_op jit(solution)/shard_map/all_to_all | solution.py:122
  315.1 1.1 fusion.23
  (78 shorter events, 8.4 us)
Async XLA Ops:
  7.2 166.1 %copy-start = (bf16[1,336,3072]{2,1,0:T(8,128)(2,1)S(1)}, bf16[1,336,3072]{2,1,0:T(8,128)(2,1)}, u32[]{:S(2)}) copy-start(bf16[1,336,3072]{2,1,0:T(8,128)(2,1)} %param.13) | copy-start | bytes 6193156
  7.2 125.4 %all-gather.5.cloned.1.call-start = ((), (), s32[]{:S(2)}) async-start(), calls=%async_computation.7 | async-start | bytes 5898240 | tf_op jit(solution)/shard_map/all_gather | solution.py:52
  61.4 2.4 copy-start.13
  63.7 109.5 %all-gather.3.cloned.1.call-start = ((), (), s32[]{:S(2)}) async-start(), calls=%async_computation.6 | async-start | bytes 5898240 | tf_op jit(solution)/shard_map/all_gather | solution.py:58
  107.5 2.6 copy-start.14
  109.9 9.7 %copy-start.6 = (s32[32,4,16]{2,1,0:T(4,128)}, s32[32,4,16]{2,1,0:T(4,128)S(1)}, u32[]{:S(2)}) copy-start(s32[32,4,16]{2,1,0:T(4,128)S(1)} %copy.89) | copy-start | bytes 24580
  110.0 9.5 %copy-start.8 = (s32[32,4,12]{2,1,0:T(4,128)}, s32[32,4,12]{2,1,0:T(4,128)S(1)}, u32[]{:S(2)}) copy-start(s32[32,4,12]{2,1,0:T(4,128)S(1)} %copy.90) | copy-start | bytes 18436
  111.3 13.1 %all-to-all-start = ((bf16[1,16,12]{2,0,1:T(2,128)(2,1)}), bf16[1,16,12]{2,0,1:T(2,128)(2,1)S(1)}, u32[]{:S(2)}, u32[]{:S(2)}) async-start(bf16[1,16,12]{2,0,1:T(2,128)(2,1)} %copy.91), calls=%async_computation | async-start | bytes 16384 | tf_op jit(solution)/shard_map/all_to_all | solution.py:49
  114.7 170.4 %reduce-scatter.4.cloned.1.call-start = ((), (), s32[]{:S(2)}) async-start(), calls=%async_computation.8 | async-start | bytes 10027008
  132.5 6.1 %copy-start.5 = (bf16[1,336,3072]{2,1,0:T(8,128)(2,1)S(1)}, bf16[1,336,3072]{2,1,0:T(8,128)(2,1)}, u32[]{:S(2)}) copy-start(bf16[1,336,3072]{2,1,0:T(8,128)(2,1)} %param.12) | copy-start | bytes 6193156
  132.5 6.1 %copy-start.15 = (bf16[1,4,192,3072]{3,2,0,1:T(8,128)(2,1)S(1)}, bf16[1,4,192,3072]{3,2,0,1:T(8,128)(2,1)}, u32[]{:S(2)}) copy-start(bf16[1,4,192,3072]{3,2,0,1:T(8,128)(2,1)} %all-gather.5.cloned.1.call-done) | copy-start | bytes 14155780
  179.1 0.8 copy-start.10
  180.2 2.7 copy-start.2
  182.9 2.6 copy-start.3
  182.9 2.6 copy-start.4
  192.8 0.7 copy-start.16
  192.8 85.4 %copy-start.12 = (bf16[336,768]{1,0:T(8,128)(2,1)S(1)}, bf16[336,768]{1,0:T(8,128)(2,1)}, u32[]{:S(2)}) copy-start(bf16[336,768]{1,0:T(8,128)(2,1)} %get-tuple-element.7) | copy-start | bytes 1548292
  256.9 30.6 %all-to-all-start.4 = ((f32[1,16,12]{2,0,1:T(1,128)}), f32[1,16,12]{2,0,1:T(1,128)S(1)}, u32[]{:S(2)}, u32[]{:S(2)}) async-start(f32[1,16,12]{2,0,1:T(1,128)} %copy.108), calls=%async_computation.4 | async-start | bytes 16384 | tf_op jit(solution)/shard_map/all_to_all | solution.py:123
  283.7 12.7 %copy-start.11 = (bf16[336,768]{1,0:T(8,128)(2,1)S(1)}, bf16[336,768]{1,0:T(8,128)(2,1)}, u32[]{:S(2)}) copy-start(bf16[336,768]{1,0:T(8,128)(2,1)} %copy-done.10) | copy-start | bytes 1548292
  287.6 27.5 %all-to-all-start.3 = ((f32[1,16,12,768]{3,0,2,1:T(1,128)}), f32[1,16,12,768]{3,0,2,1:T(1,128)S(1)}, u32[]{:S(2)}, u32[]{:S(2)}) async-start(f32[1,16,12,768]{3,0,2,1:T(1,128)} %copy.104), calls=%async_computation.3 | async-start | bytes 1179648 | tf_op jit(solution)/shard_map/all_to_all | solution.py:122
  296.4 5.6 %copy-start.17 = (f32[336,768]{1,0:T(8,128)S(1)}, f32[336,768]{1,0:T(8,128)}, u32[]{:S(2)}) copy-start(f32[336,768]{1,0:T(8,128)} %fusion.20) | copy-start | bytes 3096580
  296.4 5.6 %copy-start.18 = (f32[336,768]{1,0:T(8,128)S(1)}, f32[336,768]{1,0:T(8,128)}, u32[]{:S(2)}) copy-start(f32[336,768]{1,0:T(8,128)} %fusion.17) | copy-start | bytes 3096580
  302.0 5.7 %copy-start.7 = (s32[32,4,16]{2,1,0:T(4,128)S(1)}, s32[32,4,16]{2,1,0:T(4,128)}, u32[]{:S(2)}) copy-start(s32[32,4,16]{2,1,0:T(4,128)} %copy-done.6) | copy-start | bytes 24580
  302.0 5.7 %copy-start.9 = (s32[32,4,12]{2,1,0:T(4,128)S(1)}, s32[32,4,12]{2,1,0:T(4,128)}, u32[]{:S(2)}) copy-start(s32[32,4,12]{2,1,0:T(4,128)} %copy-done.8) | copy-start | bytes 18436
  302.0 14.2 %copy-start.1 = (bf16[1,336,3072]{2,1,0:T(8,128)(2,1)S(1)}, bf16[1,336,3072]{2,1,0:T(8,128)(2,1)}, u32[]{:S(2)}) copy-start(bf16[1,336,3072]{2,1,0:T(8,128)(2,1)} %param.13) | copy-start | bytes 6193156
Sparse Core Ops, SparseCore 0:
  63.9 51.8 all-gather.4
  117.6 55.5 all-gather.2
  192.9 92.0 reduce-scatter.3
where the time goes:
time: 324 us; the launch traced here: 323 us
  blocking collectives  161 us (50%)
  matrix products  39.8 us (12%)
  waiting for transfers between devices  39.2 us (12%)
  starting transfers between devices  33.7 us (10%)
  local copies, waits for them, and re-layouts  32.4 us (10%)
  between operations  14 us (4%)
    unnamed x1, blocking collectives  61.2 us
    all_to_all x1, blocking collectives, per_device(): lax.all_to_all(row_buffer, 'expert', split_axis=1, concat_axis=1, tiled=T...  49.7 us
    all_to_all x1, blocking collectives, per_device(): lax.all_to_all(grad_buffer, 'expert', split_axis=1, concat_axis=1, tiled=...  42.5 us
    all_gather x1, waiting for transfers between devices, per_device(): lax.all_gather(grad_buffer.reshape(local_experts, 1, spread * CAP, model_...  31.7 us
    all_to_all x1, starting transfers between devices, per_device(): lax.all_to_all(summed_terms[0], 'expert', split_axis=1, concat_axis=1, ti...  21.3 us
    another operation x4, local copies, waits for them, and re-layouts  10.9 us
    all_to_all x1, starting transfers between devices, per_device(): lax.all_to_all(summed[0], 'expert', split_axis=1, concat_axis=1, tiled=True)  8.85 us
    all_gather x1, blocking collectives, per_device(): lax.all_gather(gate_buffer.reshape(local_experts, 1, spread * CAP), 'dp',...  7.89 us
  transfers between devices with their start and end apart: 6, of which 3 were waited for; matrix products, arithmetic and copies ran while one was open for 14% of the time, Pallas kernels for 0%

commit v1 on v0

v1 whole, which is shorter than its diff:
```python
import functools

import jax
import jax.numpy as jnp
from jax import lax
from jax.experimental import pallas as pl
from jax.experimental.pallas import tpu as pltpu
from jax.sharding import PartitionSpec as P

EXPERTS = 16
TOP = 4
CAP = 12
PAD = 16
N_DP = 4
N_ETP = 4
ROWS = EXPERTS * CAP
PADDED = EXPERTS * PAD
D = 3072
COLS = D // N_ETP
LANES = 128
MESH = pl.DeviceIdType.MESH
F32 = jnp.float32
BF16 = jnp.bfloat16


def iota(shape, dim):
    return lax.broadcasted_iota(jnp.int32, shape, dim)


def compact_matrix(rows):
    r, k = iota((rows, PADDED), 0), iota((rows, PADDED), 1)
    return jnp.where(((k >> 4) * CAP + (k & 15) == r) & ((k & 15) < CAP), 1.0, 0.0).astype(BF16)


def extra_row(which):
    b, k = iota((EXPERTS, PADDED), 0), iota((EXPERTS, PADDED), 1)
    return jnp.where(k == b * PAD + CAP + which, 1.0, 0.0).astype(BF16)


def lane_spread():
    c, k = iota((LANES, PADDED), 0), iota((LANES, PADDED), 1)
    return jnp.where((k & 15) == c, 1.0, 0.0).astype(BF16)


def block_mask():
    b, k = iota((EXPERTS, PADDED), 0), iota((EXPERTS, PADDED), 1)
    return jnp.where((k >> 4) == b, 1.0, 0.0).astype(F32)


def dot(a, b):
    return jnp.dot(a, b, preferred_element_type=F32)


def dot_t(a, b):
    return lax.dot_general(a, b, (((1,), (1,)), ((), ())), preferred_element_type=F32)


def position():
    return lax.axis_index("dp"), lax.axis_index("expert"), lax.axis_index("etp")


def copy_to(src, dst, send_sem, recv_sem, device):
    return pltpu.make_async_remote_copy(
        src_ref=src, dst_ref=dst, send_sem=send_sem, recv_sem=recv_sem, device_id=device, device_id_type=MESH
    )


def greet(devices):
    barrier = pltpu.get_barrier_semaphore()
    for device in devices:
        pl.semaphore_signal(barrier, inc=1, device_id=device, device_id_type=MESH)
    pl.semaphore_wait(barrier, len(devices))


def piece(ref, i, j):
    return ref.at[i, :, pl.ds(pl.multiple_of(j * COLS, COLS), COLS)]


class PlaneGather:
    COUNT = 22

    def __init__(self, ref, dp_first, send_sems, recv_sems):
        x, e, y = position()
        self.ref, self.dp_first, self.send_sems, self.recv_sems = ref, dp_first, send_sems, recv_sems
        self.e = e
        self.a, self.b = (x, y) if dp_first else (y, x)
        self.sent = []

    def at(self, i, j, half=None):
        i, j = i % 4, j % 4
        view = piece(self.ref, i, j) if self.dp_first else piece(self.ref, j, i)
        if half is not None:
            view = view.at[pl.ds(half * (ROWS // 2), ROWS // 2), :]
        return view

    def device(self, i, j):
        i, j = i % 4, j % 4
        return (i, self.e, j) if self.dp_first else (j, self.e, i)

    def copy(self, view, index, device):
        return copy_to(view, view, self.send_sems.at[index], self.recv_sems.at[index], device)

    def send(self, view, index, device):
        c = self.copy(view, index, device)
        c.start()
        self.sent.append(c)

    def wait(self, view, index):
        self.copy(view, index, self.device(self.a, self.b)).wait_recv()

    def both_second(self, i, slot, half=None):
        view = self.at(i, self.b, half)
        self.send(view, 4 + 2 * slot, self.device(self.a, self.b + 1))
        self.send(view, 5 + 2 * slot, self.device(self.a, self.b - 1))

    def forward_second(self, i, slot):
        self.wait(self.at(i, self.b - 1), 4 + 2 * slot)
        self.send(self.at(i, self.b - 1, 0), 14 + 2 * slot, self.device(self.a, self.b + 1))
        self.wait(self.at(i, self.b + 1), 5 + 2 * slot)
        self.send(self.at(i, self.b + 1, 1), 15 + 2 * slot, self.device(self.a, self.b - 1))

    def steps(self):
        a, b = self.a, self.b

        def own():
            self.send(self.at(a, b), 0, self.device(a + 1, b))
            self.send(self.at(a, b), 1, self.device(a - 1, b))
            self.both_second(a, 0)

        def lower():
            self.wait(self.at(a - 1, b), 0)
            self.send(self.at(a - 1, b, 0), 2, self.device(a + 1, b))
            self.both_second(a - 1, 1)

        def upper():
            self.wait(self.at(a + 1, b), 1)
            self.send(self.at(a + 1, b, 1), 3, self.device(a - 1, b))
            self.both_second(a + 1, 2)

        def opposite():
            self.wait(self.at(a + 2, b, 0), 2)
            self.both_second(a + 2, 3, 0)
            self.wait(self.at(a + 2, b, 1), 3)
            self.both_second(a + 2, 4, 1)

        def opposite_second():
            self.wait(self.at(a + 2, b - 1, 0), 10)
            self.send(self.at(a + 2, b - 1, 0), 20, self.device(a, b + 1))
            self.wait(self.at(a + 2, b + 1, 1), 13)
            self.send(self.at(a + 2, b + 1, 1), 21, self.device(a, b - 1))

        def last():
            self.wait(self.at(a + 2, b + 1, 0), 11)
            self.wait(self.at(a + 2, b - 1, 1), 12)
            for slot, i in enumerate((a, a - 1, a + 1, a + 2)):
                self.wait(self.at(i, b + 2, 0), 14 + 2 * slot)
                self.wait(self.at(i, b + 2, 1), 15 + 2 * slot)

        return [
            own,
            lower,
            upper,
            lambda: self.forward_second(a, 0),
            opposite,
            lambda: self.forward_second(a - 1, 1),
            lambda: self.forward_second(a + 1, 2),
            opposite_second,
            last,
        ]


def gather_kernel(sx, sd, rows, grads, scales, rx, rd, slot_send, slot_recv, x_send, x_recv, d_send, d_recv, g_send, g_recv):
    x, e, y = position()
    peers = [(x, (e + j) % EXPERTS, y) for j in range(1, EXPERTS)]
    peers += [((x + j) % N_DP, e, y) for j in range(1, N_DP)]
    peers += [(x, e, (y + 1) % N_ETP), (x, e, (y + 3) % N_ETP)]
    greet(peers)

    slots = []
    for which, (source, landed) in enumerate(((sx, rx), (sd, rd))):
        for j in range(1, EXPERTS):
            to = (e + j) % EXPERTS
            c = copy_to(source.at[to], landed.at[e], slot_send.at[which, j], slot_recv.at[which, j], (x, to, y))
            c.start()
            slots.append(c)
        landed[e] = source[e]

    def arrive(which):
        source, landed = ((sx, rx), (sd, rd))[which]
        for j in range(1, EXPERTS):
            frm = (e + EXPERTS - j) % EXPERTS
            copy_to(source.at[frm], landed.at[frm], slot_send.at[which, j], slot_recv.at[which, j], (x, e, y)).wait_recv()

    compact = compact_matrix(ROWS)
    columns = pl.ds(pl.multiple_of(y * COLS, COLS), COLS)
    gather_x = PlaneGather(rows, True, x_send, x_recv)
    gather_d = PlaneGather(grads, False, d_send, d_recv)
    steps_x, steps_d = gather_x.steps(), gather_d.steps()

    arrive(0)
    block = rx[...].reshape(PADDED, COLS)
    rows[x, :, columns] = dot(compact, block).astype(BF16)
    steps_x[0]()
    gate = dot(extra_row(0), block[:, :LANES]).astype(BF16)
    gate = jnp.sum(dot(gate, lane_spread()) * block_mask(), axis=0, keepdims=True).astype(BF16)
    gate = dot_t(gate, compact_matrix(PADDED))
    scales[x] = jnp.broadcast_to(gate, (8, PADDED))
    sent = []
    for j in range(1, N_DP):
        c = copy_to(scales.at[x], scales.at[x], g_send.at[j], g_recv.at[j], ((x + j) % N_DP, e, y))
        c.start()
        sent.append(c)

    arrive(1)
    grads[x, :, columns] = dot(compact, rd[...].reshape(PADDED, COLS)).astype(BF16)
    steps_d[0]()
    for one, two in zip(steps_x[1:], steps_d[1:]):
        one()
        two()
    for j in range(1, N_DP):
        frm = (x + N_DP - j) % N_DP
        copy_to(scales.at[frm], scales.at[frm], g_send.at[j], g_recv.at[j], (x, e, y)).wait_recv()
    for c in slots + sent + gather_x.sent + gather_d.sent:
        c.wait_send()


class PlaneReduce:
    def __init__(self, ref, low, dp_first, opp, full, opp2, full2, sems):
        x, e, y = position()
        self.ref, self.low, self.dp_first = ref, low, dp_first
        self.opp, self.full, self.opp2, self.full2 = opp, full, opp2, full2
        self.send_sems, self.recv_sems = sems
        self.e = e
        self.a, self.b = (x, y) if dp_first else (y, x)
        self.sent = []

    def device(self, i, j):
        i, j = i % 4, j % 4
        return (i, self.e, j) if self.dp_first else (j, self.e, i)

    def at(self, i, j, start, size):
        i, j = i % 4, j % 4
        view = piece(self.ref, i, j) if self.dp_first else piece(self.ref, j, i)
        return view.at[pl.ds(self.low + start, size), :]

    def send(self, src, dst, index, device):
        c = copy_to(src, dst, self.send_sems.at[index], self.recv_sems.at[index], device)
        c.start()
        self.sent.append(c)

    def wait(self, dst, index):
        copy_to(dst, dst, self.send_sems.at[index], self.recv_sems.at[index], self.device(self.a, self.b)).wait_recv()

    HALF = ROWS // 2
    QUARTER = ROWS // 4

    def send_opposite(self, j, k):
        a, b, q = self.a, self.b, self.QUARTER
        self.send(self.at(a + 2, j, 0, q), self.opp.at[0, k], 4 * k, self.device(a + 1, b))
        self.send(self.at(a + 2, j, q, q), self.opp.at[1, k], 4 * k + 1, self.device(a - 1, b))

    def send_near(self, j, k):
        a, b, q, h = self.a, self.b, self.QUARTER, self.HALF
        for side, to in ((0, a + 1), (1, a - 1)):
            self.wait(self.opp.at[side, k], 4 * k + side)
            view = self.at(to, j, side * q, q)
            view[...] = (view[...].astype(F32) + self.opp[side, k].astype(F32)).astype(BF16)
            self.send(self.at(to, j, 0, h), self.full.at[side, k], 4 * k + 2 + side, self.device(to, b))

    def total(self, j, k):
        for side in range(2):
            self.wait(self.full.at[side, k], 4 * k + 2 + side)
        own = self.at(self.a, j, 0, self.HALF)[...].astype(F32)
        return own + self.full[0, k].astype(F32) + self.full[1, k].astype(F32)

    def steps(self):
        a, b, q, h = self.a, self.b, self.QUARTER, self.HALF
        order = (b + 2, b + 1, b - 1, b)
        second = 16

        def keep(k):
            view = self.at(a, order[k], 0, h)
            view[...] = self.total(order[k], k).astype(BF16)

        def second_opposite():
            keep(0)
            self.send(self.at(a, b + 2, 0, q), self.opp2.at[0], second, self.device(a, b + 1))
            self.send(self.at(a, b + 2, q, q), self.opp2.at[1], second + 1, self.device(a, b - 1))

        def second_near(side):
            to = b + 1 if side == 0 else b - 1
            keep(1 + side)
            self.wait(self.opp2.at[side], second + side)
            view = self.at(a, to, side * q, q)
            view[...] = (view[...].astype(F32) + self.opp2[side].astype(F32)).astype(BF16)
            self.send(self.at(a, to, 0, h), self.full2.at[side], second + 2 + side, self.device(a, to))

        def finish():
            value = self.total(b, 3)
            for side in range(2):
                self.wait(self.full2.at[side], second + 2 + side)
            return value + self.full2[0].astype(F32) + self.full2[1].astype(F32)

        steps = [functools.partial(self.send_opposite, order[k], k) for k in range(4)]
        steps += [functools.partial(self.send_near, order[k], k) for k in range(4)]
        steps += [second_opposite, lambda: second_near(0), lambda: second_near(1), finish]
        return steps


def return_kernel(slots_in, terms_in, table, out, terms_out, slots, terms, landed_x, landed_y,
                  opp_a, full_a, opp2_a, full2_a, opp_b, full_b, opp2_b, full2_b, ready, back,
                  send_a, recv_a, send_b, recv_b, t_send, t_recv, r_send, r_recv, local):
    x, e, y = position()
    load = pltpu.make_async_copy(slots_in, slots, local)
    load.start()
    terms[...] = terms_in[...]
    peers = [(x, (e + j) % EXPERTS, y) for j in range(1, EXPERTS)]
    peers += [((x + j) % N_DP, e, y) for j in range(1, N_DP)]
    peers += [(x, e, (y + j) % N_ETP) for j in range(1, N_ETP)]
    greet(peers)
    load.wait()

    one = PlaneReduce(slots, 0, True, opp_a, full_a, opp2_a, full2_a, (send_a, recv_a))
    two = PlaneReduce(slots, ROWS // 2, False, opp_b, full_b, opp2_b, full2_b, (send_b, recv_b))
    steps = list(zip(one.steps(), two.steps()))
    for first, second in steps[:4]:
        first()
        second()
    sent = []
    for j in range(1, N_DP):
        to = (x + j) % N_DP
        c = copy_to(terms.at[to], landed_x.at[j], t_send.at[j], t_recv.at[j], (to, e, y))
        c.start()
        sent.append(c)
    for first, second in steps[4:8]:
        first()
        second()
    total = terms[x]
    for j in range(1, N_DP):
        copy_to(landed_x.at[j], landed_x.at[j], t_send.at[j], t_recv.at[j], (x, e, y)).wait_recv()
        total = total + landed_x[j]
    landed_y[0] = total
    for j in range(1, N_ETP):
        c = copy_to(landed_y.at[0], landed_y.at[j], t_send.at[3 + j], t_recv.at[3 + j], (x, e, (y + j) % N_ETP))
        c.start()
        sent.append(c)
    for first, second in steps[8:11]:
        first()
        second()
    for j in range(1, N_ETP):
        copy_to(landed_y.at[j], landed_y.at[j], t_send.at[3 + j], t_recv.at[3 + j], (x, e, y)).wait_recv()
        total = total + landed_y[j]

    value = total[:1]
    spread, mask = lane_spread(), block_mask()
    widen = compact_matrix(PADDED)
    spare = jnp.zeros((PADDED, LANES), F32)
    for which in range(3):
        part = value.astype(BF16)
        value = value - part.astype(F32)
        part = (dot(part, widen) * mask).astype(BF16)
        part = dot_t(part, spread).astype(BF16)
        spare = spare + lax.dot_general(
            extra_row(which), part, (((0,), (0,)), ((), ())), preferred_element_type=F32
        )
    summed = jnp.concatenate([steps[11][0](), steps[11][1]()], axis=0).astype(BF16)
    padded = lax.dot_general(compact_matrix(ROWS), summed, (((0,), (0,)), ((), ())), preferred_element_type=F32)
    ready[:, :, :LANES] = (padded[:, :LANES] + spare).astype(BF16).reshape(EXPERTS, PAD, LANES)
    ready[:, :, LANES:] = padded[:, LANES:].astype(BF16).reshape(EXPERTS, PAD, COLS - LANES)

    for j in range(1, EXPERTS):
        to = (e + j) % EXPERTS
        c = copy_to(ready.at[to], back.at[e], r_send.at[j], r_recv.at[j], (x, to, y))
        c.start()
        sent.append(c)
    back[e] = ready[e]
    for j in range(1, EXPERTS):
        frm = (e + EXPERTS - j) % EXPERTS
        copy_to(back.at[frm], back.at[frm], r_send.at[j], r_recv.at[j], (x, e, y)).wait_recv()
    block = back[...].reshape(PADDED, COLS)
    out[...] = dot(table[...], block).astype(BF16)
    lanes = block[:, :LANES]
    terms_out[...] = dot(extra_row(0), lanes) + (dot(extra_row(1), lanes) + dot(extra_row(2), lanes))
    for c in sent + one.sent + two.sent:
        c.wait_send()


def gather_call(sx, sd):
    dma = pltpu.SemaphoreType.DMA
    vmem = pl.BlockSpec(memory_space=pltpu.VMEM)
    whole = jax.ShapeDtypeStruct((N_DP, ROWS, D), BF16)
    return pl.pallas_call(
        gather_kernel,
        out_shape=(whole, whole, jax.ShapeDtypeStruct((N_DP, 8, PADDED), F32)),
        in_specs=[vmem] * 2,
        out_specs=(vmem,) * 3,
        scratch_shapes=[
            pltpu.VMEM((EXPERTS, PAD, COLS), BF16),
            pltpu.VMEM((EXPERTS, PAD, COLS), BF16),
            dma((2, EXPERTS)),
            dma((2, EXPERTS)),
            dma((PlaneGather.COUNT,)),
            dma((PlaneGather.COUNT,)),
            dma((PlaneGather.COUNT,)),
            dma((PlaneGather.COUNT,)),
            dma((N_DP,)),
            dma((N_DP,)),
        ],
        compiler_params=pltpu.CompilerParams(collective_id=0, has_side_effects=True, vmem_limit_bytes=48 << 20),
        name="gather",
    )(sx, sd)


def return_call(slots, terms, table):
    dma = pltpu.SemaphoreType.DMA
    vmem = pl.BlockSpec(memory_space=pltpu.VMEM)
    tok = table.shape[0]
    half, quarter = ROWS // 2, ROWS // 4
    landing = [
        pltpu.VMEM((2, 4, quarter, COLS), BF16),
        pltpu.VMEM((2, 4, half, COLS), BF16),
        pltpu.VMEM((2, quarter, COLS), BF16),
        pltpu.VMEM((2, half, COLS), BF16),
    ]
    return pl.pallas_call(
        return_kernel,
        out_shape=(jax.ShapeDtypeStruct((tok, COLS), BF16), jax.ShapeDtypeStruct((EXPERTS, LANES), F32)),
        in_specs=[pl.BlockSpec(memory_space=pl.ANY), vmem, vmem],
        out_specs=(vmem, vmem),
        scratch_shapes=[
            pltpu.VMEM((N_DP, ROWS, D), BF16),
            pltpu.VMEM((N_DP, 8, PADDED), F32),
            pltpu.VMEM((N_DP, 8, PADDED), F32),
            pltpu.VMEM((N_ETP, 8, PADDED), F32),
            *landing,
            *landing,
            pltpu.VMEM((EXPERTS, PAD, COLS), BF16),
            pltpu.VMEM((EXPERTS, PAD, COLS), BF16),
            dma((20,)),
            dma((20,)),
            dma((20,)),
            dma((20,)),
            dma((8,)),
            dma((8,)),
            dma((EXPERTS,)),
            dma((EXPERTS,)),
            dma,
        ],
        compiler_params=pltpu.CompilerParams(collective_id=1, has_side_effects=True, vmem_limit_bytes=48 << 20),
        name="return",
    )(slots, terms, table)


def route(expert_ids):
    count = expert_ids.shape[0]
    flat = expert_ids.reshape(-1)
    onehot = (flat[:, None] == jnp.arange(EXPERTS, dtype=jnp.int32)).astype(BF16)
    before = jnp.tril(jnp.ones((flat.shape[0], flat.shape[0]), BF16), -1)
    earlier = dot(before, onehot)
    slot = jnp.sum(earlier * onehot.astype(F32), axis=1).astype(jnp.int32)
    hits = (onehot[:, :, None] > 0) & (slot[:, None, None] == jnp.arange(PAD, dtype=jnp.int32))
    return hits.reshape(count, TOP, EXPERTS, PAD)


def per_device(tokens, out_grad, gates, expert_ids, w_gate, w_up, w_down):
    tok = tokens.shape[0]
    y = lax.axis_index("etp")
    w_gate, w_up, w_down = w_gate[0], w_up[0], w_down[0]
    hits = route(expert_ids)
    hits_f = hits.astype(F32)
    table = jnp.sum(hits_f, axis=1).reshape(tok, PADDED).astype(BF16)
    quarter = functools.partial(lax.dynamic_slice_in_dim, start_index=y * COLS, slice_size=COLS, axis=1)
    spread = lambda rows: lax.dot_general(
        table, quarter(rows), (((0,), (0,)), ((), ())), preferred_element_type=F32
    ).reshape(EXPERTS, PAD, COLS)
    gate_rows = jnp.sum(hits_f * gates.astype(F32)[:, :, None, None], axis=(0, 1))
    sx = spread(tokens).at[:, CAP, :PAD].add(gate_rows).astype(BF16)
    sd = spread(out_grad).astype(BF16)

    rows, grads, scales = gather_call(sx, sd)
    rows, grads = rows.reshape(N_DP * ROWS, D), grads.reshape(N_DP * ROWS, D)
    scales = scales[:, 0, :ROWS].reshape(1, N_DP * ROWS)
    pre_gate, pre_up, raw_grad = dot_t(w_gate, rows), dot_t(w_up, rows), dot_t(w_down, grads)
    sigmoid_gate = jax.nn.sigmoid(pre_gate)
    activated = pre_gate * sigmoid_gate
    product = activated * pre_up
    terms = jnp.sum(product * raw_grad, axis=0)
    scaled = (scales * product).astype(BF16)
    hidden_grad = scales * raw_grad
    grad_pre_gate = (hidden_grad * pre_up * sigmoid_gate * (1.0 + pre_gate * (1.0 - sigmoid_gate))).astype(BF16)
    grad_pre_up = (hidden_grad * activated).astype(BF16)
    back = functools.partial(lax.dot_general, dimension_numbers=(((0,), (0,)), ((), ())), preferred_element_type=F32)
    slots = (back(grad_pre_gate, w_gate) + back(grad_pre_up, w_up)).astype(BF16).reshape(N_DP, ROWS, D)
    terms = jnp.pad(terms.reshape(N_DP, 1, ROWS), ((0, 0), (0, 7), (0, PADDED - ROWS)))
    grad_gate = dot(grad_pre_gate, rows).astype(BF16)
    grad_up = dot(grad_pre_up, rows).astype(BF16)
    grad_down = dot(scaled, grads).astype(BF16)

    input_grad, gate_slots = return_call(slots, terms, table)
    share = tok // N_ETP
    own = lax.dynamic_slice_in_dim(hits_f, y * share, share, 0)
    gate_grad = jnp.sum(own * gate_slots[:, :PAD], axis=(2, 3))
    return input_grad, gate_grad, grad_gate[None], grad_up[None], grad_down[None]


def solution(mesh):
    in_specs = (
        P(("dp", "expert"), None),
        P(("dp", "expert"), None),
        P(("dp", "expert"), None),
        P(("dp", "expert"), None),
        P("expert", ("dp", "etp"), None),
        P("expert", ("dp", "etp"), None),
        P("expert", ("dp", "etp"), None),
    )
    out_specs = (
        P(("dp", "expert"), "etp"),
        P(("dp", "expert", "etp"), None),
        P("expert", ("dp", "etp"), None),
        P("expert", ("dp", "etp"), None),
        P("expert", ("dp", "etp"), None),
    )
    return jax.shard_map(
        per_device, mesh=mesh, in_specs=in_specs, out_specs=out_specs, check_vma=False
    )
```

time: 324 us -> 165 us (0.51)
  blocking collectives: 161 us -> 0 us
  Pallas kernels: 0 us -> 123 us
  waiting for transfers between devices: 39.2 us -> 0 us
  starting transfers between devices: 33.7 us -> 0 us
  local copies, waits for them, and re-layouts: 32.4 us -> 7.48 us
  between operations: 14 us -> 0.82 us
  matrix products: 39.8 us -> 31.9 us
    pallas_call x0 -> x2, Pallas kernels: none -> 123 us  [the longest x1 77.6 us: gather_call(): pl.pallas_call(gather_kernel, out_shape=(whole, whole, jax.ShapeDtypeStru...]
    all_to_all x2 -> x0, blocking collectives: 92.2 us -> none  [the longest x1 49.7 us: per_device(): lax.all_to_all(row_buffer, 'expert', split_axis=1, concat_axis=1, tiled=T...]
    unnamed x1 -> x0, blocking collectives: 61.2 us -> none
    all_to_all x3 -> x0, starting transfers between devices: 33.5 us -> none  [the longest x1 21.3 us: per_device(): lax.all_to_all(summed_terms[0], 'expert', split_axis=1, concat_axis=1, ti...]
    all_gather x2 -> x0, waiting for transfers between devices: 31.7 us -> none  [the longest x1 31.7 us: per_device(): lax.all_gather(grad_buffer.reshape(local_experts, 1, spread * CAP, model_...]
    another operation x4 -> x0, local copies, waits for them, and re-layouts: 10.9 us -> none
    all_gather x1 -> x0, blocking collectives: 7.89 us -> none  [per_device(): lax.all_gather(gate_buffer.reshape(local_experts, 1, spread * CAP), 'dp',...]
    dot_general x11, matrix products: 39.8 us -> 31.9 us  [the longest x4 14.5 us: dot(): return jnp.dot(a, b, preferred_element_type=F32)]
  transfers between devices with their start and end apart: 6 -> 0, of which waited for: 3 -> 0; matrix products, arithmetic and copies ran while one was open for 14% -> 0% of each run, Pallas kernels for 0% -> 0%
where the time goes in v1:
time: 165 us
  Pallas kernels  123 us (75%)
  matrix products  31.9 us (19%)
  local copies, waits for them, and re-layouts  7.48 us (5%)
    pallas_call x1, Pallas kernels, gather_call(): pl.pallas_call(gather_kernel, out_shape=(whole, whole, jax.ShapeDtypeStru...  77.6 us
    pallas_call x1, Pallas kernels, return_call(): pl.pallas_call(return_kernel, out_shape=(jax.ShapeDtypeStruct((tok, COLS)...  45.4 us
    dot_general x4, matrix products, dot(): return jnp.dot(a, b, preferred_element_type=F32)  14.5 us
    dot_general x3, matrix products, dot_t(): lax.dot_general(a, b, (((1,), (1,)), ((), ())), preferred_element_type=F32)  9.37 us
    unnamed x22, local copies, waits for them, and re-layouts  5.82 us

profile of v1, /device:TPU:1, one launch (start us, length us, event | category | flops | bytes accessed | tf_op | source)
XLA Modules:
  0.0 164.5 jit_solution(7596022096993168393)
XLA Ops:
  0.7 0.9 copy.21
  1.6 0.1 eq.46
  1.7 0.2 fusion.21
  1.9 0.1 convert_element_type.67
  2.0 0.1 iota_compare_fusion
  2.2 0.8 copy.24
  2.9 0.6 fusion.22
  3.6 0.2 copy.28
  3.7 0.1 copy.26.table
  3.8 1.0 convolution_convert_fusion.3.sd
  4.9 1.0 fusion.28
  5.9 0.4 scatter-add.4
  6.4 0.4 and_convert_fusion
  6.8 77.6 %gather.1 = (bf16[4,192,3072]{2,1,0:T(8,128)(2,1)S(1)}, bf16[4,192,3072]{2,1,0:T(8,128)(2,1)}, f32[4,8,256]{2,1,0:T(8,128)S(1)}) custom-call(bf16[16,16,768]{2,1,0:T(8,128)(2,1)S(1)} %convert_element_type.72.sx, bf16[16,16,768]{2,1,0:T(8,128)(2,1)S(1)} %convolution_convert_fusion.3.sd), custom_call_target="tpu_custom_call" | custom-call | tf_op jit(solution)/shard_map/gather/pallas_call | solution.py:392
  84.4 2.1 %copy-done.1 = bf16[4,192,3072]{2,1,0:T(8,128)(2,1)} copy-done((bf16[4,192,3072]{2,1,0:T(8,128)(2,1)}, bf16[4,192,3072]{2,1,0:T(8,128)(2,1)S(1)}, u32[]{:S(2)}) %copy-start.1) | copy-done | bytes 4718616
  86.5 0.1 mul.69
  86.6 4.3 %fusion.18 = f32[336,768]{1,0:T(8,128)S(1)} fusion(bf16[768,3072]{1,0:T(8,128)(2,1)} %bitcast.65, bf16[1,336,3072]{2,1,0:T(8,128)(2,1)S(1)} %copy-done), kind=kOutput, calls=%fused_computation.18 | convolution fusion | flops 1585446912 | bytes 7815168 | tf_op jit(solution)/shard_map/dot_general | solution.py:55
  90.9 0.1 copy-done.3
  91.0 1.8 %fusion.15 = f32[336,768]{1,0:T(8,128)S(1)} fusion(bf16[768,3072]{1,0:T(8,128)(2,1)S(1)} %bitcast.68, bf16[1,336,3072]{2,1,0:T(8,128)(2,1)S(1)} %copy-done.3), kind=kOutput, calls=%fused_computation.17 | convolution fusion | flops 1585446912 | bytes 7815168 | tf_op jit(solution)/shard_map/dot_general | solution.py:55
  92.9 0.5 copy-done.7
  93.4 0.7 copy-done.8
  94.0 3.3 %multiply_reduce_fusion = (f32[768]{0:T(1024)S(1)}, bf16[336,768]{1,0:T(8,128)(2,1)}, bf16[336,768]{1,0:T(8,128)(2,1)}) fusion(f32[336,768]{1,0:T(8,128)S(1)} %fusion.15, f32[336,768]{1,0:T(8,128)S(1)} %fusion.18, f32[768]{0:T(1024)S(1)} %mul.69, bf16[768,3072]{1,0:T(8,128)(2,1)S(1)} %bitcast.71, bf16[1,336,3072]{2,1,0:T(8,128)(2,1)S(1)} %copy-done.8), kind=kOutput, calls=%fused_computation.26 | convolution fusion | flops 1589832960 | bytes 9885696 | tf_op jit(solution)/shard_map/dot_general | solution.py:55
  97.3 3.2 %fusion.2 = bf16[1,336,3072]{2,1,0:T(8,128)(2,1)} fusion(bf16[768,3072]{1,0:T(8,128)(2,1)S(1)} %bitcast.72, f32[768]{0:T(1024)S(1)} %mul.69, f32[336,768]{1,0:T(8,128)S(1)} %fusion.15, f32[336,768]{1,0:T(8,128)S(1)} %fusion.18), kind=kOutput, calls=%fused_computation.6 | convolution fusion | flops 1588285440 | bytes 8850432 | tf_op jit(solution)/shard_map/dot_general | solution.py:51
  100.5 0.1 reshape.131
  100.6 5.6 %fusion = bf16[1,336,3072]{2,1,0:T(8,128)(2,1)} fusion(bf16[336,768]{1,0:T(8,128)(2,1)} %get-tuple-element.35, bf16[768,3072]{1,0:T(8,128)(2,1)} %bitcast.66), kind=kOutput, calls=%fused_computation.4 | convolution fusion | flops 1586479104 | bytes 7299072 | tf_op jit(solution)/shard_map/dot_general | solution.py:51
  106.2 5.5 %fusion.1 = bf16[1,336,3072]{2,1,0:T(8,128)(2,1)} fusion(bf16[336,768]{1,0:T(8,128)(2,1)S(1)} %copy-done.5, bf16[768,3072]{1,0:T(8,128)(2,1)} %bitcast.67), kind=kOutput, calls=%fused_computation.5 | convolution fusion | flops 1586479104 | bytes 7299072 | tf_op jit(solution)/shard_map/dot_general | solution.py:51
  111.7 2.9 %fusion.3 = f32[768,3072]{1,0:T(8,128)S(1)} fusion(bf16[336,768]{1,0:T(8,128)(2,1)S(1)} %copy-done.6, bf16[1,336,3072]{2,1,0:T(8,128)(2,1)S(1)} %copy-done), kind=kOutput, calls=%fused_computation.7 | convolution fusion | flops 1585446912 | bytes 12017664 | tf_op jit(solution)/shard_map/dot_general | solution.py:493
  114.6 3.1 %add_convert_fusion = bf16[768,3072]{1,0:T(8,128)(2,1)S(1)} fusion(f32[768,3072]{1,0:T(8,128)S(1)} %fusion.3, bf16[336,768]{1,0:T(8,128)(2,1)S(1)} %copy-done.5, bf16[1,336,3072]{2,1,0:T(8,128)(2,1)S(1)} %copy-done.4), kind=kOutput, calls=%fused_computation | convolution fusion | flops 1590165504 | bytes 16736256 | tf_op jit(solution)/shard_map/dot_general | solution.py:493
  117.6 45.4 %return.1 = (bf16[32,768]{1,0:T(8,128)(2,1)S(1)}, f32[16,128]{1,0:T(8,128)S(1)}) custom-call(bf16[4,192,3072]{2,1,0:T(8,128)(2,1)S(1)} %bitcast.63, f32[4,8,256]{2,1,0:T(8,128)S(1)} %pad.8.terms_in, bf16[32,256]{1,0:T(8,128)(2,1)S(1)} %copy.26.table), custom_call_target="tpu_custom_call" | custom-call | tf_op jit(solution)/shard_map/return/pallas_call | solution.py:425
  163.1 0.1 multiply_reduce_fusion.1
  163.2 0.7 copy.27
  163.9 0.6 copy.32
  (20 shorter events, 0.1 us)
Async XLA Ops:
  0.6 86.0 %copy-start = (bf16[1,336,3072]{2,1,0:T(8,128)(2,1)S(1)}, bf16[1,336,3072]{2,1,0:T(8,128)(2,1)}, u32[]{:S(2)}) copy-start(bf16[1,336,3072]{2,1,0:T(8,128)(2,1)} %param.13) | copy-start | bytes 6193156
  84.4 2.1 %copy-start.1 = (bf16[4,192,3072]{2,1,0:T(8,128)(2,1)}, bf16[4,192,3072]{2,1,0:T(8,128)(2,1)S(1)}, u32[]{:S(2)}) copy-start(bf16[4,192,3072]{2,1,0:T(8,128)(2,1)S(1)} %get-tuple-element.24) | copy-start | bytes 14155780
  86.6 4.3 %copy-start.2 = (bf16[4,192,3072]{2,1,0:T(8,128)(2,1)S(1)}, bf16[4,192,3072]{2,1,0:T(8,128)(2,1)}, u32[]{:S(2)}) copy-start(bf16[4,192,3072]{2,1,0:T(8,128)(2,1)} %copy-done.1) | copy-start | bytes 14155780
  86.6 4.4 %copy-start.3 = (bf16[1,336,3072]{2,1,0:T(8,128)(2,1)S(1)}, bf16[1,336,3072]{2,1,0:T(8,128)(2,1)}, u32[]{:S(2)}) copy-start(bf16[1,336,3072]{2,1,0:T(8,128)(2,1)} %param.14) | copy-start | bytes 6193156
  91.0 2.3 %copy-start.7 = (bf16[4,192,3072]{2,1,0:T(8,128)(2,1)S(1)}, bf16[4,192,3072]{2,1,0:T(8,128)(2,1)}, u32[]{:S(2)}) copy-start(bf16[4,192,3072]{2,1,0:T(8,128)(2,1)} %get-tuple-element.23) | copy-start | bytes 14155780
  91.0 3.0 %copy-start.8 = (bf16[1,336,3072]{2,1,0:T(8,128)(2,1)S(1)}, bf16[1,336,3072]{2,1,0:T(8,128)(2,1)}, u32[]{:S(2)}) copy-start(bf16[1,336,3072]{2,1,0:T(8,128)(2,1)} %param.15) | copy-start | bytes 6193156
  100.6 5.6 %copy-start.5 = (bf16[336,768]{1,0:T(8,128)(2,1)S(1)}, bf16[336,768]{1,0:T(8,128)(2,1)}, u32[]{:S(2)}) copy-start(bf16[336,768]{1,0:T(8,128)(2,1)} %get-tuple-element.36) | copy-start | bytes 1548292
  106.2 5.5 %copy-start.6 = (bf16[336,768]{1,0:T(8,128)(2,1)S(1)}, bf16[336,768]{1,0:T(8,128)(2,1)}, u32[]{:S(2)}) copy-start(bf16[336,768]{1,0:T(8,128)(2,1)} %get-tuple-element.35) | copy-start | bytes 1548292
  111.7 2.9 %copy-start.4 = (bf16[1,336,3072]{2,1,0:T(8,128)(2,1)S(1)}, bf16[1,336,3072]{2,1,0:T(8,128)(2,1)}, u32[]{:S(2)}) copy-start(bf16[1,336,3072]{2,1,0:T(8,128)(2,1)} %param.14) | copy-start | bytes 6193156

commit v2 on v1

v2 whole, which is shorter than its diff:
```python
import jax
import jax.numpy as jnp
from jax import lax
from jax.experimental import pallas as pl
from jax.experimental.pallas import tpu as pltpu
from jax.sharding import PartitionSpec as P

EXPERTS = 16
TOP = 4
CAP = 12
PAD = 16
N_DP = 4
N_ETP = 4
ROWS = EXPERTS * CAP
PADDED = EXPERTS * PAD
D = 3072
FF = 336
FPAD = 384
COLS = D // N_ETP
LANES = 128
MESH = pl.DeviceIdType.MESH
F32 = jnp.float32
BF16 = jnp.bfloat16


def iota(shape, dim):
    return lax.broadcasted_iota(jnp.int32, shape, dim)


def compact_matrix(rows):
    r, k = iota((rows, PADDED), 0), iota((rows, PADDED), 1)
    return jnp.where(((k >> 4) * CAP + (k & 15) == r) & ((k & 15) < CAP), 1.0, 0.0).astype(BF16)


def extra_row(which):
    b, k = iota((EXPERTS, PADDED), 0), iota((EXPERTS, PADDED), 1)
    return jnp.where(k == b * PAD + CAP + which, 1.0, 0.0).astype(BF16)


def lane_spread():
    c, k = iota((LANES, PADDED), 0), iota((LANES, PADDED), 1)
    return jnp.where((k & 15) == c, 1.0, 0.0).astype(BF16)


def block_mask():
    b, k = iota((EXPERTS, PADDED), 0), iota((EXPERTS, PADDED), 1)
    return jnp.where((k >> 4) == b, 1.0, 0.0).astype(F32)


def block_of_row():
    r, b = iota((ROWS, EXPERTS), 0), iota((ROWS, EXPERTS), 1)
    return jnp.where((r >= b * CAP) & (r < b * CAP + CAP), 1.0, 0.0).astype(BF16)


def slot_of_row():
    return dot_t(compact_matrix(ROWS), lane_spread())


def parts(value):
    out = []
    for _ in range(3):
        part = value.astype(BF16)
        value = value - part.astype(F32)
        out.append(part)
    return out


def dot(a, b):
    return jnp.dot(a, b, preferred_element_type=F32)


def dot_t(a, b):
    return lax.dot_general(a, b, (((1,), (1,)), ((), ())), preferred_element_type=F32)


def t_dot(a, b):
    return lax.dot_general(a, b, (((0,), (0,)), ((), ())), preferred_element_type=F32)


def position():
    return lax.axis_index("dp"), lax.axis_index("expert"), lax.axis_index("etp")


def copy_to(src, dst, send_sem, recv_sem, device):
    return pltpu.make_async_remote_copy(
        src_ref=src, dst_ref=dst, send_sem=send_sem, recv_sem=recv_sem, device_id=device, device_id_type=MESH
    )


def piece(ref, i, j):
    return ref.at[i, :, pl.ds(pl.multiple_of(j * COLS, COLS), COLS)]


class PlaneGather:
    COUNT = 22

    def __init__(self, ref, dp_first, send_sems, recv_sems):
        x, e, y = position()
        self.ref, self.dp_first, self.send_sems, self.recv_sems = ref, dp_first, send_sems, recv_sems
        self.e = e
        self.a, self.b = (x, y) if dp_first else (y, x)
        self.sent = []

    def at(self, i, j, half=None):
        i, j = i % 4, j % 4
        view = piece(self.ref, i, j) if self.dp_first else piece(self.ref, j, i)
        if half is not None:
            view = view.at[pl.ds(half * (ROWS // 2), ROWS // 2), :]
        return view

    def device(self, i, j):
        i, j = i % 4, j % 4
        return (i, self.e, j) if self.dp_first else (j, self.e, i)

    def copy(self, view, index, device):
        return copy_to(view, view, self.send_sems.at[index], self.recv_sems.at[index], device)

    def send(self, view, index, device):
        c = self.copy(view, index, device)
        c.start()
        self.sent.append(c)

    def wait(self, view, index):
        self.copy(view, index, self.device(self.a, self.b)).wait_recv()

    def both_second(self, i, slot, half=None):
        view = self.at(i, self.b, half)
        self.send(view, 4 + 2 * slot, self.device(self.a, self.b + 1))
        self.send(view, 5 + 2 * slot, self.device(self.a, self.b - 1))

    def forward_second(self, i, slot):
        self.wait(self.at(i, self.b - 1), 4 + 2 * slot)
        self.send(self.at(i, self.b - 1, 0), 14 + 2 * slot, self.device(self.a, self.b + 1))
        self.wait(self.at(i, self.b + 1), 5 + 2 * slot)
        self.send(self.at(i, self.b + 1, 1), 15 + 2 * slot, self.device(self.a, self.b - 1))

    def steps(self):
        a, b = self.a, self.b

        def own():
            self.send(self.at(a, b), 0, self.device(a + 1, b))
            self.send(self.at(a, b), 1, self.device(a - 1, b))
            self.both_second(a, 0)

        def lower():
            self.wait(self.at(a - 1, b), 0)
            self.send(self.at(a - 1, b, 0), 2, self.device(a + 1, b))
            self.both_second(a - 1, 1)

        def upper():
            self.wait(self.at(a + 1, b), 1)
            self.send(self.at(a + 1, b, 1), 3, self.device(a - 1, b))
            self.both_second(a + 1, 2)

        def opposite():
            self.wait(self.at(a + 2, b, 0), 2)
            self.both_second(a + 2, 3, 0)
            self.wait(self.at(a + 2, b, 1), 3)
            self.both_second(a + 2, 4, 1)

        def opposite_second():
            self.wait(self.at(a + 2, b - 1, 0), 10)
            self.send(self.at(a + 2, b - 1, 0), 20, self.device(a, b + 1))
            self.wait(self.at(a + 2, b + 1, 1), 13)
            self.send(self.at(a + 2, b + 1, 1), 21, self.device(a, b - 1))

        return [
            own,
            lower,
            upper,
            lambda: self.forward_second(a, 0),
            opposite,
            lambda: self.forward_second(a - 1, 1),
            lambda: self.forward_second(a + 1, 2),
            opposite_second,
        ]

    def finish_first(self, slot):
        a, b = self.a, self.b
        if slot == 3:
            self.wait(self.at(a + 2, b + 1, 0), 11)
            self.wait(self.at(a + 2, b - 1, 1), 12)
        i = (a, a - 1, a + 1, a + 2)[slot]
        self.wait(self.at(i, b + 2, 0), 14 + 2 * slot)
        self.wait(self.at(i, b + 2, 1), 15 + 2 * slot)

    def finish_second(self, slot):
        a, b = self.a, self.b
        if slot == 1:
            self.wait(self.at(a + 2, b - 1, 1), 12)
        if slot == 2:
            self.wait(self.at(a + 2, b + 1, 0), 11)
        if slot == 3:
            for k, i in enumerate((a, a - 1, a + 1, a + 2)):
                self.wait(self.at(i, b + 2, 0), 14 + 2 * k)
                self.wait(self.at(i, b + 2, 1), 15 + 2 * k)


class PlaneReduce:
    HALF = ROWS // 2
    QUARTER = ROWS // 4
    COUNT = 20

    def __init__(self, ref, out, low, dp_first, order, opp, full, opp2, full2, send_sems, recv_sems):
        x, e, y = position()
        self.ref, self.out, self.low, self.dp_first, self.order = ref, out, low, dp_first, order
        self.opp, self.full, self.opp2, self.full2 = opp, full, opp2, full2
        self.send_sems, self.recv_sems = send_sems, recv_sems
        self.e = e
        self.a, self.b = (x, y) if dp_first else (y, x)
        self.sent = []

    def device(self, i, j):
        i, j = i % 4, j % 4
        return (i, self.e, j) if self.dp_first else (j, self.e, i)

    def at(self, i, j, start, size, ref=None):
        i, j = i % 4, j % 4
        ref = self.out if ref is None else ref
        view = piece(ref, i, j) if self.dp_first else piece(ref, j, i)
        return view.at[pl.ds(self.low + start, size), :]

    def send(self, src, dst, index, device):
        c = copy_to(src, dst, self.send_sems.at[index], self.recv_sems.at[index], device)
        c.start()
        self.sent.append(c)

    def wait(self, dst, index):
        copy_to(dst, dst, self.send_sems.at[index], self.recv_sems.at[index], self.device(self.a, self.b)).wait_recv()

    def opposite(self, k):
        a, b, q = self.a, self.b, self.QUARTER
        j = b + self.order[k]
        self.send(self.at(a + 2, j, 0, q), self.opp.at[0, k], 4 * k, self.device(a + 1, b))
        self.send(self.at(a + 2, j, q, q), self.opp.at[1, k], 4 * k + 1, self.device(a - 1, b))

    def near(self, k):
        a, b, q, h = self.a, self.b, self.QUARTER, self.HALF
        j = b + self.order[k]
        for side, to in ((0, a + 1), (1, a - 1)):
            self.wait(self.opp.at[side, k], 4 * k + side)
            own = self.at(to, j, side * q, q, self.ref)[...]
            self.at(to, j, side * q, q)[...] = (own + self.opp[side, k].astype(F32)).astype(BF16)
            self.send(self.at(to, j, 0, h), self.full.at[side, k], 4 * k + 2 + side, self.device(to, b))

    def total(self, relative):
        k = self.order.index(relative)
        for side in range(2):
            self.wait(self.full.at[side, k], 4 * k + 2 + side)
        own = self.at(self.a, self.b + relative, 0, self.HALF, self.ref)[...]
        return own + self.full[0, k].astype(F32) + self.full[1, k].astype(F32)

    def second_opposite(self):
        a, b, q, h = self.a, self.b, self.QUARTER, self.HALF
        self.at(a, b + 2, 0, h)[...] = self.total(2).astype(BF16)
        self.send(self.at(a, b + 2, 0, q), self.opp2.at[0], 16, self.device(a, b + 1))
        self.send(self.at(a, b + 2, q, q), self.opp2.at[1], 17, self.device(a, b - 1))

    def second_near(self, side):
        a, b, q, h = self.a, self.b, self.QUARTER, self.HALF
        step = 1 if side == 0 else -1
        value = self.total(step)
        self.wait(self.opp2.at[side], 16 + side)
        extra = self.opp2[side].astype(F32)
        if side == 0:
            value = jnp.concatenate([value[:q] + extra, value[q:]], axis=0)
        else:
            value = jnp.concatenate([value[:q], value[q:] + extra], axis=0)
        self.at(a, b + step, 0, h)[...] = value.astype(BF16)
        self.send(self.at(a, b + step, 0, h), self.full2.at[side], 18 + side, self.device(a, b + step))

    def finish(self):
        value = self.total(0)
        for side in range(2):
            self.wait(self.full2.at[side], 18 + side)
        return value + self.full2[0].astype(F32) + self.full2[1].astype(F32)


def kernel(
    tokens, out_grad, gates, expert_ids, w_gate, w_up, w_down,
    input_grad, gate_grad, grad_gate, grad_up, grad_down,
    tok, cot, sx, sd, rx, rd, rows, grads, scales, w_in, w_out, pre, raw, deltas, scaled, turned, turned_scaled,
    sums, wire, made, terms, landed_x, landed_y,
    opp_a, full_a, opp2_a, full2_a, opp_b, full_b, opp2_b, full2_b, back, pairs,
    slot_send, slot_recv, x_send, x_recv, d_send, d_recv, g_send, g_recv,
    send_a, recv_a, send_b, recv_b, t_send, t_recv, r_send, r_recv, local,
):
    x, e, y = position()
    columns = pl.ds(pl.multiple_of(y * COLS, COLS), COLS)
    loads = [
        pltpu.make_async_copy(tokens.at[:, columns], tok, local.at[0]),
        pltpu.make_async_copy(out_grad.at[:, columns], cot, local.at[1]),
        pltpu.make_async_copy(w_gate.at[0], w_in.at[pl.ds(0, FF), :], local.at[2]),
        pltpu.make_async_copy(w_up.at[0], w_in.at[pl.ds(FPAD, FF), :], local.at[3]),
        pltpu.make_async_copy(w_down.at[0], w_out.at[pl.ds(0, FF), :], local.at[4]),
    ]
    for c in loads:
        c.start()
    peers = [(x, (e + j) % EXPERTS, y) for j in range(1, EXPERTS)]
    peers += [((x + j) % N_DP, e, y) for j in range(1, N_DP)]
    peers += [(x, e, (y + j) % N_ETP) for j in range(1, N_ETP)]
    barrier = pltpu.get_barrier_semaphore()
    for device in peers:
        pl.semaphore_signal(barrier, inc=1, device_id=device, device_id_type=MESH)

    count = tok.shape[0]
    lane = iota((count, PADDED), 1)
    ids, weight = expert_ids[...], gates[...].astype(F32)
    chosen = [jnp.where(ids[:, k : k + 1] == (lane >> 4), 1.0, 0.0) for k in range(TOP)]
    member = chosen[0] + chosen[1] + chosen[2] + chosen[3]
    before = jnp.where(iota((count, count), 0) > iota((count, count), 1), 1.0, 0.0).astype(BF16)
    earlier = dot(before, member.astype(BF16))
    table = jnp.where(earlier == (lane & 15).astype(F32), member, 0.0)
    gate_slots = sum(chosen[k] * weight[:, k : k + 1] for k in range(TOP)) * table
    gate_slots = jnp.sum(gate_slots, axis=0, keepdims=True)
    gate_rows = dot_t((block_mask() * gate_slots).astype(BF16), lane_spread()).astype(BF16)
    gate_rows = t_dot(extra_row(0), gate_rows)
    table = table.astype(BF16)

    loads[0].wait()
    slots = t_dot(table, tok[...])
    sx[:, :, :LANES] = (slots[:, :LANES] + gate_rows).astype(BF16).reshape(EXPERTS, PAD, LANES)
    sx[:, :, LANES:] = slots[:, LANES:].astype(BF16).reshape(EXPERTS, PAD, COLS - LANES)
    pl.semaphore_wait(barrier, len(peers))
    sent = []

    def exchange(which):
        source, landed = ((sx, rx), (sd, rd))[which]
        for j in range(1, EXPERTS):
            to = (e + j) % EXPERTS
            c = copy_to(source.at[to], landed.at[e], slot_send.at[which, j], slot_recv.at[which, j], (x, to, y))
            c.start()
            sent.append(c)
        landed[e] = source[e]

    def arrive(which):
        source, landed = ((sx, rx), (sd, rd))[which]
        for j in range(1, EXPERTS):
            frm = (e + EXPERTS - j) % EXPERTS
            copy_to(source.at[frm], landed.at[frm], slot_send.at[which, j], slot_recv.at[which, j], (x, e, y)).wait_recv()

    exchange(0)
    loads[1].wait()
    sd[...] = t_dot(table, cot[...]).astype(BF16).reshape(EXPERTS, PAD, COLS)
    exchange(1)
    for ref, low in ((w_in, FF), (w_in, FPAD + FF), (w_out, FF)):
        ref[pl.ds(low, FPAD - FF), :] = jnp.zeros((FPAD - FF, D), BF16)

    gather_x = PlaneGather(rows, True, x_send, x_recv)
    gather_d = PlaneGather(grads, False, d_send, d_recv)
    steps_x, steps_d = gather_x.steps(), gather_d.steps()
    compact = compact_matrix(ROWS)
    arrive(0)
    block = rx[...].reshape(PADDED, COLS)
    rows[x, :, columns] = dot(compact, block).astype(BF16)
    steps_x[0]()
    scales[x] = dot(extra_row(0), block[:, :LANES]).astype(BF16)
    for j in range(1, N_DP):
        c = copy_to(scales.at[x], scales.at[x], g_send.at[j], g_recv.at[j], ((x + j) % N_DP, e, y))
        c.start()
        sent.append(c)
    arrive(1)
    grads[x, :, columns] = dot(compact, rd[...].reshape(PADDED, COLS)).astype(BF16)
    steps_d[0]()

    reduce_a = PlaneReduce(
        sums, wire, 0, True, (2, 1, -1, 0), opp_a, full_a, opp2_a, full2_a, send_a, recv_a
    )
    reduce_b = PlaneReduce(
        sums, wire, ROWS // 2, False, (0, -1, 1, 2), opp_b, full_b, opp2_b, full2_b, send_b, recv_b
    )

    def group(slot):
        g = (x + (0, 3, 1, 2)[slot]) % N_DP
        gather_x.finish_first(slot)
        gather_d.finish_second(slot)
        if slot == 0:
            for c in loads[2:]:
                c.wait()
        else:
            j = (0, 3, 1, 2)[slot]
            copy_to(scales.at[g], scales.at[g], g_send.at[4 - j], g_recv.at[4 - j], (x, e, y)).wait_recv()
        pre[...] = jnp.zeros_like(pre)
        raw[...] = jnp.zeros_like(raw)

        @pl.loop(0, N_ETP)
        def _(k):
            part = pl.ds(pl.multiple_of(k * COLS, COLS), COLS)
            pre[...] += dot_t(rows[g, :, part], w_in[:, part])
            raw[...] += dot_t(grads[g, :, part], w_out[:, part])

        a, u, r = pre[:, :FPAD], pre[:, FPAD:], raw[...]
        which = slot_of_row()
        scale = jnp.sum(dot(block_of_row(), scales[g]) * which, axis=1, keepdims=True)
        sigmoid = jax.nn.sigmoid(a)
        activated = a * sigmoid
        product = activated * u
        q = jnp.sum(product * r, axis=1, keepdims=True) * which
        terms[g] = sum(t_dot(block_of_row(), part) for part in parts(q))
        own = pl.ds(pl.multiple_of(g * ROWS, ROWS), ROWS)
        scaled[own, :] = (scale * product).astype(BF16)
        hidden = scale * r
        deltas[own, :FPAD] = (hidden * u * sigmoid * (1.0 + a * (1.0 - sigmoid))).astype(BF16)
        deltas[own, FPAD:] = (hidden * activated).astype(BF16)

        @pl.loop(0, N_ETP)
        def _(k):
            part = pl.ds(pl.multiple_of(k * COLS, COLS), COLS)
            value = dot(deltas[own, :], w_in[:, part])
            sums[g, :, part] = value
            wire[g, :, part] = value.astype(BF16)

    def weight_grad(which):
        source = (rows, rows, grads)[which]

        @pl.loop(0, N_ETP)
        def _(k):
            part = pl.ds(pl.multiple_of(k * COLS, COLS), COLS)
            left = turned_scaled[:FF, :] if which == 2 else turned[pl.ds(which * FPAD, FF), :]
            made[which, :, part] = dot(left, source[:, :, part].reshape(N_DP * ROWS, COLS)).astype(BF16)

        c = pltpu.make_async_copy(made.at[which], (grad_gate, grad_up, grad_down)[which].at[0], local.at[5 + which])
        c.start()
        loads.append(c)

    for one, two in zip(steps_x[1:6], steps_d[1:6]):
        one()
        two()
    group(0)
    for one, two in zip(steps_x[6:], steps_d[6:]):
        one()
        two()
    reduce_b.opposite(0)
    group(1)
    reduce_b.opposite(1)
    reduce_b.near(0)
    group(2)
    reduce_b.opposite(2)
    reduce_b.near(1)
    group(3)
    for k in range(4):
        reduce_a.opposite(k)
    reduce_b.opposite(3)
    reduce_b.near(2)
    for j in range(1, N_DP):
        to = (x + j) % N_DP
        c = copy_to(terms.at[to], landed_x.at[j], t_send.at[j], t_recv.at[j], (to, e, y))
        c.start()
        sent.append(c)
    turned[...] = deltas[...].T
    turned_scaled[...] = scaled[...].T
    reduce_a.near(0)
    reduce_b.near(3)
    for k in range(1, 4):
        reduce_a.near(k)
    weight_grad(0)
    total = terms[x]
    for j in range(1, N_DP):
        copy_to(landed_x.at[j], landed_x.at[j], t_send.at[j], t_recv.at[j], (x, e, y)).wait_recv()
        total = total + landed_x[j]
    landed_y[0] = total
    for j in range(1, N_ETP):
        c = copy_to(landed_y.at[0], landed_y.at[j], t_send.at[3 + j], t_recv.at[3 + j], (x, e, (y + j) % N_ETP))
        c.start()
        sent.append(c)
    reduce_a.second_opposite()
    reduce_b.second_opposite()
    weight_grad(1)
    for side in range(2):
        reduce_a.second_near(side)
        reduce_b.second_near(side)
    weight_grad(2)
    for j in range(1, N_ETP):
        copy_to(landed_y.at[j], landed_y.at[j], t_send.at[3 + j], t_recv.at[3 + j], (x, e, y)).wait_recv()
        total = total + landed_y[j]
    spare = sum(t_dot(extra_row(which), part) for which, part in enumerate(parts(total)))
    summed = jnp.concatenate([reduce_a.finish(), reduce_b.finish()], axis=0).astype(BF16)
    padded = t_dot(compact, summed)
    for c in sent[: 2 * (EXPERTS - 1)]:
        c.wait_send()
    sx[:, :, :LANES] = (padded[:, :LANES] + spare).astype(BF16).reshape(EXPERTS, PAD, LANES)
    sx[:, :, LANES:] = padded[:, LANES:].astype(BF16).reshape(EXPERTS, PAD, COLS - LANES)
    for j in range(1, EXPERTS):
        to = (e + j) % EXPERTS
        c = copy_to(sx.at[to], back.at[e], r_send.at[j], r_recv.at[j], (x, to, y))
        c.start()
        sent.append(c)
    back[e] = sx[e]
    for j in range(1, EXPERTS):
        frm = (e + EXPERTS - j) % EXPERTS
        copy_to(back.at[frm], back.at[frm], r_send.at[j], r_recv.at[j], (x, e, y)).wait_recv()
    block = back[...].reshape(PADDED, COLS)
    input_grad[...] = dot(table, block).astype(BF16)
    lanes = block[:, :LANES]
    value = jnp.zeros((EXPERTS, PADDED), F32)
    for which in range(3):
        part = dot(extra_row(which), lanes).astype(BF16)
        value = value + dot(part, lane_spread())
    value = jnp.sum(value * block_mask(), axis=0, keepdims=True) * table.astype(F32)
    for k in range(TOP):
        pairs[:, k : k + 1] = jnp.sum(chosen[k] * value, axis=1, keepdims=True)
    share = gate_grad.shape[0]
    gate_grad[...] = pairs[pl.ds(pl.multiple_of(y * share, share), share), :]
    for c in loads[5:]:
        c.wait()
    for c in sent[2 * (EXPERTS - 1) :] + gather_x.sent + gather_d.sent + reduce_a.sent + reduce_b.sent:
        c.wait_send()


def per_device(tokens, out_grad, gates, expert_ids, w_gate, w_up, w_down):
    dma = pltpu.SemaphoreType.DMA
    vmem = pl.BlockSpec(memory_space=pltpu.VMEM)
    hbm = pl.BlockSpec(memory_space=pl.ANY)
    count = tokens.shape[0]
    half, quarter = ROWS // 2, ROWS // 4
    landing = [
        pltpu.VMEM((2, 4, quarter, COLS), BF16),
        pltpu.VMEM((2, 4, half, COLS), BF16),
        pltpu.VMEM((2, quarter, COLS), BF16),
        pltpu.VMEM((2, half, COLS), BF16),
    ]
    all_rows = N_DP * ROWS
    weight = jax.ShapeDtypeStruct(w_gate.shape, BF16)
    return pl.pallas_call(
        kernel,
        out_shape=(
            jax.ShapeDtypeStruct((count, COLS), BF16),
            jax.ShapeDtypeStruct((count // N_ETP, TOP), F32),
            weight,
            weight,
            weight,
        ),
        in_specs=[hbm, hbm, vmem, vmem, hbm, hbm, hbm],
        out_specs=(vmem, vmem, hbm, hbm, hbm),
        scratch_shapes=[
            pltpu.VMEM((count, COLS), BF16),
            pltpu.VMEM((count, COLS), BF16),
            *[pltpu.VMEM((EXPERTS, PAD, COLS), BF16)] * 4,
            pltpu.VMEM((N_DP, ROWS, D), BF16),
            pltpu.VMEM((N_DP, ROWS, D), BF16),
            pltpu.VMEM((N_DP, EXPERTS, LANES), BF16),
            pltpu.VMEM((2 * FPAD, D), BF16),
            pltpu.VMEM((FPAD, D), BF16),
            pltpu.VMEM((ROWS, 2 * FPAD), F32),
            pltpu.VMEM((ROWS, FPAD), F32),
            pltpu.VMEM((all_rows, 2 * FPAD), BF16),
            pltpu.VMEM((all_rows, FPAD), BF16),
            pltpu.VMEM((2 * FPAD, all_rows), BF16),
            pltpu.VMEM((FPAD, all_rows), BF16),
            pltpu.VMEM((N_DP, ROWS, D), F32),
            pltpu.VMEM((N_DP, ROWS, D), BF16),
            pltpu.VMEM((3, FF, D), BF16),
            pltpu.VMEM((N_DP, EXPERTS, LANES), F32),
            pltpu.VMEM((N_DP, EXPERTS, LANES), F32),
            pltpu.VMEM((N_ETP, EXPERTS, LANES), F32),
            *landing,
            *landing,
            pltpu.VMEM((EXPERTS, PAD, COLS), BF16),
            pltpu.VMEM((count, TOP), F32),
            dma((2, EXPERTS)),
            dma((2, EXPERTS)),
            *[dma((PlaneGather.COUNT,))] * 4,
            dma((N_DP,)),
            dma((N_DP,)),
            *[dma((PlaneReduce.COUNT,))] * 4,
            dma((8,)),
            dma((8,)),
            dma((EXPERTS,)),
            dma((EXPERTS,)),
            dma((8,)),
        ],
        compiler_params=pltpu.CompilerParams(collective_id=0, has_side_effects=True, vmem_limit_bytes=58 << 20),
        name="backward",
    )(tokens, out_grad, gates, expert_ids, w_gate, w_up, w_down)


def solution(mesh):
    in_specs = (
        P(("dp", "expert"), None),
        P(("dp", "expert"), None),
        P(("dp", "expert"), None),
        P(("dp", "expert"), None),
        P("expert", ("dp", "etp"), None),
        P("expert", ("dp", "etp"), None),
        P("expert", ("dp", "etp"), None),
    )
    out_specs = (
        P(("dp", "expert"), "etp"),
        P(("dp", "expert", "etp"), None),
        P("expert", ("dp", "etp"), None),
        P("expert", ("dp", "etp"), None),
        P("expert", ("dp", "etp"), None),
    )
    return jax.shard_map(
        per_device, mesh=mesh, in_specs=in_specs, out_specs=out_specs, check_vma=False
    )
```

time: 165 us -> 140 us (0.85)
  matrix products: 31.9 us -> 0 us
  local copies, waits for them, and re-layouts: 7.48 us -> 12.3 us
  Pallas kernels: 123 us -> 127 us
    dot_general x11 -> x0, matrix products: 31.9 us -> none  [the longest x4 14.5 us: dot(): return jnp.dot(a, b, preferred_element_type=F32)]
    unnamed x22 -> x10, local copies, waits for them, and re-layouts: 5.82 us -> 10.9 us
    pallas_call x2 -> x1, Pallas kernels: 123 us -> 127 us  [per_device(): pl.pallas_call(kernel, out_shape=(jax.ShapeDtypeStruct((count, COLS), BF1...]
where the time goes in v2:
time: 140 us
  Pallas kernels  127 us (91%)
  local copies, waits for them, and re-layouts  12.3 us (9%)
    pallas_call x1, Pallas kernels, per_device(): pl.pallas_call(kernel, out_shape=(jax.ShapeDtypeStruct((count, COLS), BF1...  127 us
    unnamed x10, local copies, waits for them, and re-layouts  10.9 us

profile of v2, /device:TPU:1, one launch (start us, length us, event | category | flops | bytes accessed | tf_op | source)
XLA Modules:
  0.0 139.9 jit_solution(9447050067507108832)
XLA Ops:
  0.6 1.4 copy.12.gates
  2.0 1.4 copy.13.expert_ids
  3.4 127.0 %backward.1 = (bf16[32,768]{1,0:T(8,128)(2,1)}, f32[8,4]{1,0:T(8,128)}, bf16[1,336,3072]{2,1,0:T(8,128)(2,1)}, bf16[1,336,3072]{2,1,0:T(8,128)(2,1)}, bf16[1,336,3072]{2,1,0:T(8,128)(2,1)}) custom-call(bf16[32,3072]{1,0:T(8,128)(2,1)} %tokens.1, bf16[32,3072]{1,0:T(8,128)(2,1)} %out_grad.1, bf16[32,4]{1,0:T(8,128)(2,1)} %copy.12.gates, ...), custom_call_target="tpu_custom_call" | custom-call | tf_op jit(solution)/shard_map/backward/pallas_call | solution.py:524
  130.4 1.3 copy.14
  131.7 1.4 %copy.19 = bf16[32,768]{1,0:T(8,128)(2,1)} copy(bf16[32,768]{1,0:T(8,128)(2,1)} %get-tuple-element.15) | data formatting | bytes 98304
  133.1 0.0 copy-start.1
  133.1 3.2 %copy.20 = bf16[1,336,3072]{2,1,0:T(8,128)(2,1)} copy(bf16[1,336,3072]{2,1,0:T(8,128)(2,1)} %get-tuple-element.17) | data formatting | bytes 4128768
  136.3 0.0 copy-done.1
  136.3 0.0 copy-start
  136.3 1.3 copy.21
  137.6 1.0 copy-done
  138.6 1.3 copy.22
Async XLA Ops:
  133.1 3.2 %copy-start.1 = (bf16[1,336,3072]{2,1,0:T(8,128)(2,1)S(1)}, bf16[1,336,3072]{2,1,0:T(8,128)(2,1)}, u32[]{:S(2)}) copy-start(bf16[1,336,3072]{2,1,0:T(8,128)(2,1)} %get-tuple-element.18) | copy-start | bytes 6193156
  136.3 2.3 %copy-start = (bf16[1,336,3072]{2,1,0:T(8,128)(2,1)S(1)}, bf16[1,336,3072]{2,1,0:T(8,128)(2,1)}, u32[]{:S(2)}) copy-start(bf16[1,336,3072]{2,1,0:T(8,128)(2,1)} %get-tuple-element.19) | copy-start | bytes 6193156

commit v3 on v2

--- a/solution.py
+++ b/solution.py
@@ -17,6 +17,12 @@
 FF = 336
 FPAD = 384
 COLS = D // N_ETP
+WHOLE = 512
+SLOTTED = D - WHOLE
+PART = SLOTTED // N_ETP
+EARLY = 256
+TOK = 32
+CHUNK = 512
 LANES = 128
 MESH = pl.DeviceIdType.MESH
 F32 = jnp.float32
@@ -32,6 +38,11 @@
     return jnp.where(((k >> 4) * CAP + (k & 15) == r) & ((k & 15) < CAP), 1.0, 0.0).astype(BF16)
 
 
+def same_row(which):
+    k, m = iota((PADDED, PADDED), 0), iota((PADDED, PADDED), 1)
+    return jnp.where(m == (k >> 4) * PAD + CAP + which, 1.0, 0.0).astype(BF16)
+
+
 def extra_row(which):
     b, k = iota((EXPERTS, PADDED), 0), iota((EXPERTS, PADDED), 1)
     return jnp.where(k == b * PAD + CAP + which, 1.0, 0.0).astype(BF16)
@@ -40,11 +51,6 @@
 def lane_spread():
     c, k = iota((LANES, PADDED), 0), iota((LANES, PADDED), 1)
     return jnp.where((k & 15) == c, 1.0, 0.0).astype(BF16)
-
-
-def block_mask():
-    b, k = iota((EXPERTS, PADDED), 0), iota((EXPERTS, PADDED), 1)
-    return jnp.where((k >> 4) == b, 1.0, 0.0).astype(F32)
 
 
 def block_of_row():
@@ -94,19 +100,22 @@
 class PlaneGather:
     COUNT = 22
 
-    def __init__(self, ref, dp_first, send_sems, recv_sems):
+    def __init__(self, ref, start, width, dp_first, send_sems, recv_sems):
         x, e, y = position()
         self.ref, self.dp_first, self.send_sems, self.recv_sems = ref, dp_first, send_sems, recv_sems
+        self.start, self.width = start, width
         self.e = e
         self.a, self.b = (x, y) if dp_first else (y, x)
         self.sent = []
 
     def at(self, i, j, half=None):
         i, j = i % 4, j % 4
-        view = piece(self.ref, i, j) if self.dp_first else piece(self.ref, j, i)
-        if half is not None:
-            view = view.at[pl.ds(half * (ROWS // 2), ROWS // 2), :]
-        return view
+        if not self.dp_first:
+            i, j = j, i
+        columns = pl.ds(pl.multiple_of(j * PART + self.start, LANES), self.width)
+        if half is None:
+            return self.ref.at[i, :, columns]
+        return self.ref.at[i, pl.ds(half * (ROWS // 2), ROWS // 2), columns]
 
     def device(self, i, j):
         i, j = i % 4, j % 4
@@ -276,17 +285,106 @@
         return value + self.full2[0].astype(F32) + self.full2[1].astype(F32)
 
 
+class TokenGather:
+    def __init__(self, ref, sources, dp_send, dp_recv, z_send, z_recv, core_send, core_recv, local):
+        self.x, self.e, self.y = position()
+        self.ref, self.sources = ref, sources
+        self.dp_send, self.dp_recv = dp_send, dp_recv
+        self.z_send, self.z_recv, self.core_send, self.core_recv = z_send, z_recv, core_send, core_recv
+        self.other = self.e + 1 - 2 * (self.e % 2)
+        self.sent = []
+        own = [
+            pltpu.make_async_copy(s.at[:, pl.ds(SLOTTED, WHOLE)], self.landing(self.x, which), local.at[which])
+            for which, s in enumerate(sources)
+        ]
+        self.own = own
+
+    def landing(self, i, which):
+        rows = pl.ds(pl.multiple_of(self.e * TOK, TOK), TOK)
+        return self.ref.at[i, rows, pl.ds(which * WHOLE, WHOLE)]
+
+    def block(self, e, half=None):
+        rows = pl.ds(pl.multiple_of((e % EXPERTS) * TOK, TOK), TOK)
+        if half is None:
+            return self.ref.at[:, rows, :]
+        return self.ref.at[pl.ds(2 * half, 2), rows, :]
+
+    def copy(self, src, dst, send, recv, device):
+        c = copy_to(src, dst, send, recv, device)
+        c.start()
+        self.sent.append(c)
+
+    def along_dp(self):
+        for c in self.own:
+            c.start()
+        for j in range(1, N_DP):
+            for which, source in enumerate(self.sources):
+                self.copy(
+                    source.at[:, pl.ds(SLOTTED, WHOLE)], self.landing(self.x, which),
+                    self.dp_send.at[which, j], self.dp_recv.at[which, j], ((self.x + j) % N_DP, self.e, self.y),
+                )
+
+    def arrived_dp(self):
+        for c in self.own:
+            c.wait()
+        for j in range(1, N_DP):
+            for which in range(2):
+                view = self.landing((self.x + N_DP - j) % N_DP, which)
+                copy_to(
+                    view, view, self.dp_send.at[which, j], self.dp_recv.at[which, j], (self.x, self.e, self.y)
+                ).wait_recv()
+
+    def view(self, e, side, distance):
+        away = 2 * distance
+        return self.block(e + (EXPERTS - away if side == 0 else away), side if distance == 4 else None)
+
+    def onward(self, side, distance):
+        e = self.e
+        view = self.view(e, side, distance)
+        if distance > 0:
+            copy_to(
+                view, view, self.z_send.at[side, distance], self.z_recv.at[side, distance], (self.x, e, self.y)
+            ).wait_recv()
+        if distance < 4:
+            to = (e + (2 if side == 0 else EXPERTS - 2)) % EXPERTS
+            next_view = self.view(to, side, distance + 1)
+            self.copy(
+                next_view, next_view,
+                self.z_send.at[side, distance + 1], self.z_recv.at[side, distance + 1], (self.x, to, self.y),
+            )
+        if distance > 0 or side == 0:
+            self.copy(
+                view, view, self.core_send.at[side, distance], self.core_recv.at[side, distance],
+                (self.x, self.other, self.y),
+            )
+
+    def round(self, distance):
+        for side in range(2):
+            self.onward(side, distance)
+
+    def finish(self):
+        for distance in range(5):
+            for side in range(2):
+                if distance > 0 or side == 0:
+                    view = self.view(self.other, side, distance)
+                    copy_to(
+                        view, view, self.core_send.at[side, distance], self.core_recv.at[side, distance],
+                        (self.x, self.e, self.y),
+                    ).wait_recv()
+
+
 def kernel(
     tokens, out_grad, gates, expert_ids, w_gate, w_up, w_down,
     input_grad, gate_grad, grad_gate, grad_up, grad_down,
-    tok, cot, sx, sd, rx, rd, rows, grads, scales, w_in, w_out, pre, raw, deltas, scaled, turned, turned_scaled,
+    tok, cot, sx, sd, rx, rd, rows, grads, tables, whole, w_in, w_out, pre, raw, deltas, scaled, turned, turned_scaled,
     sums, wire, made, terms, landed_x, landed_y,
-    opp_a, full_a, opp2_a, full2_a, opp_b, full_b, opp2_b, full2_b, back, pairs,
-    slot_send, slot_recv, x_send, x_recv, d_send, d_recv, g_send, g_recv,
+    opp_a, full_a, opp2_a, full2_a, opp_b, full_b, opp2_b, full2_b, back, ready,
+    slot_send, slot_recv, x_send, x_recv, late_send, late_recv, d_send, d_recv, g_send, g_recv,
+    dp_send, dp_recv, z_send, z_recv, core_send, core_recv,
     send_a, recv_a, send_b, recv_b, t_send, t_recv, r_send, r_recv, local,
 ):
     x, e, y = position()
-    columns = pl.ds(pl.multiple_of(y * COLS, COLS), COLS)
+    columns = pl.ds(pl.multiple_of(y * PART, LANES), PART)
     loads = [
         pltpu.make_async_copy(tokens.at[:, columns], tok, local.at[0]),
         pltpu.make_async_copy(out_grad.at[:, columns], cot, local.at[1]),
@@ -303,65 +401,100 @@
     for device in peers:
         pl.semaphore_signal(barrier, inc=1, device_id=device, device_id_type=MESH)
 
-    count = tok.shape[0]
-    lane = iota((count, PADDED), 1)
+    expert, place = iota((PADDED, TOK), 0) >> 4, iota((PADDED, TOK), 0) & 15
     ids, weight = expert_ids[...], gates[...].astype(F32)
-    chosen = [jnp.where(ids[:, k : k + 1] == (lane >> 4), 1.0, 0.0) for k in range(TOP)]
+    chosen = [jnp.where(ids[k : k + 1, :] == expert, 1.0, 0.0) for k in range(TOP)]
     member = chosen[0] + chosen[1] + chosen[2] + chosen[3]
-    before = jnp.where(iota((count, count), 0) > iota((count, count), 1), 1.0, 0.0).astype(BF16)
-    earlier = dot(before, member.astype(BF16))
-    table = jnp.where(earlier == (lane & 15).astype(F32), member, 0.0)
-    gate_slots = sum(chosen[k] * weight[:, k : k + 1] for k in range(TOP)) * table
-    gate_slots = jnp.sum(gate_slots, axis=0, keepdims=True)
-    gate_rows = dot_t((block_mask() * gate_slots).astype(BF16), lane_spread()).astype(BF16)
-    gate_rows = t_dot(extra_row(0), gate_rows)
+    before = jnp.where(iota((TOK, TOK), 0) < iota((TOK, TOK), 1), 1.0, 0.0).astype(BF16)
+    earlier = dot(member.astype(BF16), before)
+    table = jnp.where((earlier == place.astype(F32)) & (place < CAP), member, 0.0)
+    gate_slots = sum(chosen[k] * weight[k : k + 1, :] for k in range(TOP)) * table
+    gate_slots = jnp.sum(gate_slots, axis=1, keepdims=True)
     table = table.astype(BF16)
+    widen = jnp.where(iota((TOK, LANES), 0) == iota((TOK, LANES), 1), 1.0, 0.0).astype(BF16)
+    sent = []
 
     loads[0].wait()
-    slots = t_dot(table, tok[...])
-    sx[:, :, :LANES] = (slots[:, :LANES] + gate_rows).astype(BF16).reshape(EXPERTS, PAD, LANES)
-    sx[:, :, LANES:] = slots[:, LANES:].astype(BF16).reshape(EXPERTS, PAD, COLS - LANES)
+    sx[:, :, :PART] = dot(table, tok[...]).astype(BF16).reshape(EXPERTS, PAD, PART)
+    wide = jnp.where(iota((PADDED, LANES), 1) == TOK, gate_slots, dot(table, widen))
+    sx[:, :, PART:] = wide.astype(BF16).reshape(EXPERTS, PAD, LANES)
     pl.semaphore_wait(barrier, len(peers))
-    sent = []
+    cuts = ((sx, rx, 0, EARLY), (sx, rx, EARLY, PART + LANES - EARLY), (sd, rd, 0, PART))
 
     def exchange(which):
-        source, landed = ((sx, rx), (sd, rd))[which]
+        source, landed, start, width = cuts[which]
         for j in range(1, EXPERTS):
             to = (e + j) % EXPERTS
-            c = copy_to(source.at[to], landed.at[e], slot_send.at[which, j], slot_recv.at[which, j], (x, to, y))
+            c = copy_to(
+                source.at[to, :, pl.ds(start, width)], landed.at[e, :, pl.ds(start, width)],
+                slot_send.at[which, j], slot_recv.at[which, j], (x, to, y),
+            )
             c.start()
             sent.append(c)
-        landed[e] = source[e]
 
     def arrive(which):
-        source, landed = ((sx, rx), (sd, rd))[which]
+        source, landed, start, width = cuts[which]
         for j in range(1, EXPERTS):
             frm = (e + EXPERTS - j) % EXPERTS
-            copy_to(source.at[frm], landed.at[frm], slot_send.at[which, j], slot_recv.at[which, j], (x, e, y)).wait_recv()
-
+            view = landed.at[frm, :, pl.ds(start, width)]
+            copy_to(view, view, slot_send.at[which, j], slot_recv.at[which, j], (x, e, y)).wait_recv()
+
+    token_gather = TokenGather(
+        whole, (tokens, out_grad), dp_send, dp_recv, z_send, z_recv, core_send, core_recv, local.at[pl.ds(8, 2)]
+    )
     exchange(0)
+    token_gather.along_dp()
+    exchange(1)
+    rx[e] = sx[e]
     loads[1].wait()
-    sd[...] = t_dot(table, cot[...]).astype(BF16).reshape(EXPERTS, PAD, COLS)
-    exchange(1)
+    sd[...] = dot(table, cot[...]).astype(BF16).reshape(EXPERTS, PAD, PART)
+    exchange(2)
+    rd[e] = sd[e]
     for ref, low in ((w_in, FF), (w_in, FPAD + FF), (w_out, FF)):
         ref[pl.ds(low, FPAD - FF), :] = jnp.zeros((FPAD - FF, D), BF16)
 
-    gather_x = PlaneGather(rows, True, x_send, x_recv)
-    gather_d = PlaneGather(grads, False, d_send, d_recv)
-    steps_x, steps_d = gather_x.steps(), gather_d.steps()
+    first = PlaneGather(rows, 0, EARLY, True, x_send, x_recv)
+    late = PlaneGather(rows, EARLY, PART - EARLY, True, late_send, late_recv)
+    second = PlaneGather(grads, 0, PART, False, d_send, d_recv)
+    steps_0, steps_1, steps_2 = first.steps(), late.steps(), second.steps()
     compact = compact_matrix(ROWS)
+
+    def pack(landed, ref, start, width):
+        value = dot(compact, landed[:, :, start : start + width].reshape(PADDED, width)).astype(BF16)
+        ref[x, :, pl.ds(pl.multiple_of(y * PART + start, LANES), width)] = value
+
+    def run(steps, *which):
+        for k in which:
+            steps[k]()
+
     arrive(0)
-    block = rx[...].reshape(PADDED, COLS)
-    rows[x, :, columns] = dot(compact, block).astype(BF16)
-    steps_x[0]()
-    scales[x] = dot(extra_row(0), block[:, :LANES]).astype(BF16)
+    pack(rx, rows, 0, EARLY)
+    run(steps_0, 0)
+    token_gather.arrived_dp()
+    token_gather.round(0)
+    arrive(1)
+    pack(rx, rows, EARLY, PART - EARLY)
+    run(steps_1, 0)
+    tables[x] = dot(compact, rx[:, :, PART:].reshape(PADDED, LANES)).astype(BF16)
     for j in range(1, N_DP):
-        c = copy_to(scales.at[x], scales.at[x], g_send.at[j], g_recv.at[j], ((x + j) % N_DP, e, y))
+        c = copy_to(tables.at[x], tables.at[x], g_send.at[j], g_recv.at[j], ((x + j) % N_DP, e, y))
         c.start()
         sent.append(c)
-    arrive(1)
-    grads[x, :, columns] = dot(compact, rd[...].reshape(PADDED, COLS)).astype(BF16)
-    steps_d[0]()
+    run(steps_0, 1, 2)
+    arrive(2)
+    pack(rd, grads, 0, PART)
+    run(steps_2, 0)
+    run(steps_0, 3, 4)
+    run(steps_1, 1, 2)
+    token_gather.round(1)
+    run(steps_2, 1, 2)
+    run(steps_1, 3, 4)
+    run(steps_0, 5, 6, 7)
+    token_gather.round(2)
+    run(steps_2, 3, 4)
+    run(steps_1, 5, 6, 7)
+    token_gather.round(3)
+    run(steps_2, 5, 6, 7)
 
     reduce_a = PlaneReduce(
         sums, wire, 0, True, (2, 1, -1, 0), opp_a, full_a, opp2_a, full2_a, send_a, recv_a
@@ -370,28 +503,42 @@
         sums, wire, ROWS // 2, False, (0, -1, 1, 2), opp_b, full_b, opp2_b, full2_b, send_b, recv_b
     )
 
-    def group(slot):
-        g = (x + (0, 3, 1, 2)[slot]) % N_DP
-        gather_x.finish_first(slot)
-        gather_d.finish_second(slot)
+    def forward(g, k):
+        part = pl.ds(pl.multiple_of(k * CHUNK, CHUNK), CHUNK)
+        pre[g] += dot_t(rows[g, :, part], w_in[:, part])
+        raw[g] += dot_t(grads[g, :, part], w_out[:, part])
+
+    def begin(slot):
+        j = (0, 3, 1, 2)[slot]
+        g = (x + j) % N_DP
+        first.finish_first(slot)
+        late.finish_first(slot)
+        second.finish_second(slot)
         if slot == 0:
             for c in loads[2:]:
                 c.wait()
-        else:
-            j = (0, 3, 1, 2)[slot]
-            copy_to(scales.at[g], scales.at[g], g_send.at[4 - j], g_recv.at[4 - j], (x, e, y)).wait_recv()
-        pre[...] = jnp.zeros_like(pre)
-        raw[...] = jnp.zeros_like(raw)
-
-        @pl.loop(0, N_ETP)
+        pre[g] = jnp.zeros((ROWS, 2 * FPAD), F32)
+        raw[g] = jnp.zeros((ROWS, FPAD), F32)
+
+        @pl.loop(0, SLOTTED // CHUNK)
         def _(k):
-            part = pl.ds(pl.multiple_of(k * COLS, COLS), COLS)
-            pre[...] += dot_t(rows[g, :, part], w_in[:, part])
-            raw[...] += dot_t(grads[g, :, part], w_out[:, part])
-
-        a, u, r = pre[:, :FPAD], pre[:, FPAD:], raw[...]
+            forward(g, k)
+
+    def complete(slot):
+        j = (0, 3, 1, 2)[slot]
+        g = (x + j) % N_DP
+        if slot > 0:
+            copy_to(tables.at[g], tables.at[g], g_send.at[4 - j], g_recv.at[4 - j], (x, e, y)).wait_recv()
+        repeat = jnp.where(iota((LANES, EXPERTS * TOK), 0) == (iota((LANES, EXPERTS * TOK), 1) & 31), 1.0, 0.0)
+        within = jnp.where(iota((EXPERTS, EXPERTS * TOK), 0) == (iota((EXPERTS, EXPERTS * TOK), 1) >> 5), 1.0, 0.0)
+        pick = dot(tables[g], repeat.astype(BF16)) * dot(block_of_row(), within.astype(BF16))
+        picked = dot(pick.astype(BF16), whole[g]).astype(BF16)
+        rows[g, :, SLOTTED:] = picked[:, :WHOLE]
+        grads[g, :, SLOTTED:] = picked[:, WHOLE:]
+        forward(g, SLOTTED // CHUNK)
+        a, u, r = pre[g, :, :FPAD], pre[g, :, FPAD:], raw[g]
         which = slot_of_row()
-        scale = jnp.sum(dot(block_of_row(), scales[g]) * which, axis=1, keepdims=True)
+        scale = tables[g, :, TOK : TOK + 1].astype(F32)
         sigmoid = jax.nn.sigmoid(a)
         activated = a * sigmoid
         product = activated * u
@@ -423,21 +570,21 @@
         c.start()
         loads.append(c)
 
-    for one, two in zip(steps_x[1:6], steps_d[1:6]):
-        one()
-        two()
-    group(0)
-    for one, two in zip(steps_x[6:], steps_d[6:]):
-        one()
-        two()
+    begin(0)
+    token_gather.round(4)
+    begin(1)
+    token_gather.finish()
+    complete(0)
     reduce_b.opposite(0)
-    group(1)
+    complete(1)
     reduce_b.opposite(1)
     reduce_b.near(0)
-    group(2)
+    begin(2)
+    complete(2)
     reduce_b.opposite(2)
     reduce_b.near(1)
-    group(3)
+    begin(3)
+    complete(3)
     for k in range(4):
         reduce_a.opposite(k)
     reduce_b.opposite(3)
@@ -476,34 +623,30 @@
     spare = sum(t_dot(extra_row(which), part) for which, part in enumerate(parts(total)))
     summed = jnp.concatenate([reduce_a.finish(), reduce_b.finish()], axis=0).astype(BF16)
     padded = t_dot(compact, summed)
-    for c in sent[: 2 * (EXPERTS - 1)]:
-        c.wait_send()
-    sx[:, :, :LANES] = (padded[:, :LANES] + spare).astype(BF16).reshape(EXPERTS, PAD, LANES)
-    sx[:, :, LANES:] = padded[:, LANES:].astype(BF16).reshape(EXPERTS, PAD, COLS - LANES)
+    ready[:, :, :LANES] = (padded[:, :LANES] + spare).astype(BF16).reshape(EXPERTS, PAD, LANES)
+    ready[:, :, LANES:] = padded[:, LANES:].astype(BF16).reshape(EXPERTS, PAD, COLS - LANES)
     for j in range(1, EXPERTS):
         to = (e + j) % EXPERTS
-        c = copy_to(sx.at[to], back.at[e], r_send.at[j], r_recv.at[j], (x, to, y))
+        c = copy_to(ready.at[to], back.at[e], r_send.at[j], r_recv.at[j], (x, to, y))
         c.start()
         sent.append(c)
-    back[e] = sx[e]
+    back[e] = ready[e]
     for j in range(1, EXPERTS):
         frm = (e + EXPERTS - j) % EXPERTS
         copy_to(back.at[frm], back.at[frm], r_send.at[j], r_recv.at[j], (x, e, y)).wait_recv()
     block = back[...].reshape(PADDED, COLS)
-    input_grad[...] = dot(table, block).astype(BF16)
+    input_grad[...] = t_dot(table, block).astype(BF16)
     lanes = block[:, :LANES]
-    value = jnp.zeros((EXPERTS, PADDED), F32)
-    for which in range(3):
-        part = dot(extra_row(which), lanes).astype(BF16)
-        value = value + dot(part, lane_spread())
-    value = jnp.sum(value * block_mask(), axis=0, keepdims=True) * table.astype(F32)
-    for k in range(TOP):
-        pairs[:, k : k + 1] = jnp.sum(chosen[k] * value, axis=1, keepdims=True)
-    share = gate_grad.shape[0]
-    gate_grad[...] = pairs[pl.ds(pl.multiple_of(y * share, share), share), :]
+    mine = jnp.where(iota((PADDED, LANES), 1) == (iota((PADDED, LANES), 0) & 15), 1.0, 0.0)
+    value = sum(dot(same_row(which), lanes) for which in range(3))
+    value = jnp.sum(value * mine, axis=1, keepdims=True) * table.astype(F32)
+    pairs = jnp.concatenate([jnp.sum(chosen[k] * value, axis=0, keepdims=True) for k in range(TOP)], axis=0)
+    share = TOK // N_ETP
+    take = jnp.where(iota((TOK, share), 0) == iota((TOK, share), 1) + y * share, 1.0, 0.0).astype(BF16)
+    gate_grad[...] = sum(dot(part, take) for part in parts(pairs))
     for c in loads[5:]:
         c.wait()
-    for c in sent[2 * (EXPERTS - 1) :] + gather_x.sent + gather_d.sent + reduce_a.sent + reduce_b.sent:
+    for c in sent + first.sent + late.sent + second.sent + token_gather.sent + reduce_a.sent + reduce_b.sent:
         c.wait_send()
 
 
@@ -521,11 +664,11 @@
     ]
     all_rows = N_DP * ROWS
     weight = jax.ShapeDtypeStruct(w_gate.shape, BF16)
-    return pl.pallas_call(
+    input_grad, gate_grad, *weight_grads = pl.pallas_call(
         kernel,
         out_shape=(
             jax.ShapeDtypeStruct((count, COLS), BF16),
-            jax.ShapeDtypeStruct((count // N_ETP, TOP), F32),
+            jax.ShapeDtypeStruct((TOP, count // N_ETP), F32),
             weight,
             weight,
             weight,
@@ -533,16 +676,20 @@
         in_specs=[hbm, hbm, vmem, vmem, hbm, hbm, hbm],
         out_specs=(vmem, vmem, hbm, hbm, hbm),
         scratch_shapes=[
-            pltpu.VMEM((count, COLS), BF16),
-            pltpu.VMEM((count, COLS), BF16),
-            *[pltpu.VMEM((EXPERTS, PAD, COLS), BF16)] * 4,
+            pltpu.VMEM((count, PART), BF16),
+            pltpu.VMEM((count, PART), BF16),
+            pltpu.VMEM((EXPERTS, PAD, PART + LANES), BF16),
+            pltpu.VMEM((EXPERTS, PAD, PART), BF16),
+            pltpu.VMEM((EXPERTS, PAD, PART + LANES), BF16),
+            pltpu.VMEM((EXPERTS, PAD, PART), BF16),
             pltpu.VMEM((N_DP, ROWS, D), BF16),
             pltpu.VMEM((N_DP, ROWS, D), BF16),
-            pltpu.VMEM((N_DP, EXPERTS, LANES), BF16),
+            pltpu.VMEM((N_DP, ROWS, LANES), BF16),
+            pltpu.VMEM((N_DP, EXPERTS * TOK, 2 * WHOLE), BF16),
             pltpu.VMEM((2 * FPAD, D), BF16),
             pltpu.VMEM((FPAD, D), BF16),
-            pltpu.VMEM((ROWS, 2 * FPAD), F32),
-            pltpu.VMEM((ROWS, FPAD), F32),
+            pltpu.VMEM((N_DP, ROWS, 2 * FPAD), F32),
+            pltpu.VMEM((N_DP, ROWS, FPAD), F32),
             pltpu.VMEM((all_rows, 2 * FPAD), BF16),
             pltpu.VMEM((all_rows, FPAD), BF16),
             pltpu.VMEM((2 * FPAD, all_rows), BF16),
@@ -556,22 +703,25 @@
             *landing,
             *landing,
             pltpu.VMEM((EXPERTS, PAD, COLS), BF16),
-            pltpu.VMEM((count, TOP), F32),
-            dma((2, EXPERTS)),
-            dma((2, EXPERTS)),
-            *[dma((PlaneGather.COUNT,))] * 4,
+            pltpu.VMEM((EXPERTS, PAD, COLS), BF16),
+            dma((3, EXPERTS)),
+            dma((3, EXPERTS)),
+            *[dma((PlaneGather.COUNT,))] * 6,
             dma((N_DP,)),
             dma((N_DP,)),
+            *[dma((2, N_DP))] * 2,
+            *[dma((2, 5))] * 4,
             *[dma((PlaneReduce.COUNT,))] * 4,
             dma((8,)),
             dma((8,)),
             dma((EXPERTS,)),
             dma((EXPERTS,)),
-            dma((8,)),
+            dma((10,)),
         ],
         compiler_params=pltpu.CompilerParams(collective_id=0, has_side_effects=True, vmem_limit_bytes=58 << 20),
         name="backward",
-    )(tokens, out_grad, gates, expert_ids, w_gate, w_up, w_down)
+    )(tokens, out_grad, gates.T, expert_ids.T, w_gate, w_up, w_down)
+    return input_grad, gate_grad.T, *weight_grads
 
 
 def solution(mesh):

time: 140 us -> 137 us (0.979)
  local copies, waits for them, and re-layouts: 12.3 us -> 9.47 us
    unnamed x10 -> x9, local copies, waits for them, and re-layouts: 10.9 us -> 9.47 us
where the time goes in v3:
time: 137 us
  Pallas kernels  127 us (93%)
  local copies, waits for them, and re-layouts  9.47 us (7%)
    pallas_call x1, Pallas kernels, per_device(): pl.pallas_call(kernel, out_shape=(jax.ShapeDtypeStruct((count, COLS), BF1...  127 us
    unnamed x9, local copies, waits for them, and re-layouts  9.47 us

profile of v3, /device:TPU:1, one launch (start us, length us, event | category | flops | bytes accessed | tf_op | source)
XLA Modules:
  0.0 137.1 jit_solution(4169524532993186095)
XLA Ops:
  0.6 127.0 %backward.1 = (bf16[32,768]{1,0:T(8,128)(2,1)}, f32[4,8]{1,0:T(4,128)}, bf16[1,336,3072]{2,1,0:T(8,128)(2,1)}, bf16[1,336,3072]{2,1,0:T(8,128)(2,1)}, bf16[1,336,3072]{2,1,0:T(8,128)(2,1)}) custom-call(bf16[32,3072]{1,0:T(8,128)(2,1)} %tokens.1, bf16[32,3072]{1,0:T(8,128)(2,1)} %out_grad.1, bf16[4,32]{1,0:T(4,128)(2,1)} %bitcast.5, s32[4,32]{1,0:T(4,128)} %bitcast.3, ...), custom_call_target="tpu_custom_call" | custom-call | tf_op jit(solution)/shard_map/backward/pallas_call | solution.py:667
  127.6 1.4 %copy.17 = bf16[32,768]{1,0:T(8,128)(2,1)} copy(bf16[32,768]{1,0:T(8,128)(2,1)} %get-tuple-element.20) | data formatting | bytes 98304
  129.1 1.3 copy.18
  130.3 0.0 copy-start.1
  130.3 3.2 %copy.19 = bf16[1,336,3072]{2,1,0:T(8,128)(2,1)} copy(bf16[1,336,3072]{2,1,0:T(8,128)(2,1)} %get-tuple-element.22) | data formatting | bytes 4128768
  133.5 0.0 copy-done.1
  133.5 0.0 copy-start
  133.5 1.3 copy.20
  134.8 1.0 copy-done
  135.8 1.3 copy.21
Async XLA Ops:
  130.3 3.2 %copy-start.1 = (bf16[1,336,3072]{2,1,0:T(8,128)(2,1)S(1)}, bf16[1,336,3072]{2,1,0:T(8,128)(2,1)}, u32[]{:S(2)}) copy-start(bf16[1,336,3072]{2,1,0:T(8,128)(2,1)} %get-tuple-element.23) | copy-start | bytes 6193156
  133.5 2.3 %copy-start = (bf16[1,336,3072]{2,1,0:T(8,128)(2,1)S(1)}, bf16[1,336,3072]{2,1,0:T(8,128)(2,1)}, u32[]{:S(2)}) copy-start(bf16[1,336,3072]{2,1,0:T(8,128)(2,1)} %get-tuple-element.24) | copy-start | bytes 6193156

commit v4 on v3

--- a/solution.py
+++ b/solution.py
@@ -20,9 +20,7 @@
 WHOLE = 512
 SLOTTED = D - WHOLE
 PART = SLOTTED // N_ETP
-EARLY = 256
 TOK = 32
-CHUNK = 512
 LANES = 128
 MESH = pl.DeviceIdType.MESH
 F32 = jnp.float32
@@ -184,25 +182,15 @@
             opposite_second,
         ]
 
-    def finish_first(self, slot):
+    def finish_near(self):
         a, b = self.a, self.b
-        if slot == 3:
-            self.wait(self.at(a + 2, b + 1, 0), 11)
-            self.wait(self.at(a + 2, b - 1, 1), 12)
-        i = (a, a - 1, a + 1, a + 2)[slot]
-        self.wait(self.at(i, b + 2, 0), 14 + 2 * slot)
-        self.wait(self.at(i, b + 2, 1), 15 + 2 * slot)
-
-    def finish_second(self, slot):
-        a, b = self.a, self.b
-        if slot == 1:
-            self.wait(self.at(a + 2, b - 1, 1), 12)
-        if slot == 2:
-            self.wait(self.at(a + 2, b + 1, 0), 11)
-        if slot == 3:
-            for k, i in enumerate((a, a - 1, a + 1, a + 2)):
-                self.wait(self.at(i, b + 2, 0), 14 + 2 * k)
-                self.wait(self.at(i, b + 2, 1), 15 + 2 * k)
+        self.wait(self.at(a + 2, b + 1, 0), 11)
+        self.wait(self.at(a + 2, b - 1, 1), 12)
+
+    def finish_far(self, slot):
+        i = self.a + (0, -1, 1, 2)[slot]
+        self.wait(self.at(i, self.b + 2, 0), 14 + 2 * slot)
+        self.wait(self.at(i, self.b + 2, 1), 15 + 2 * slot)
 
 
 class PlaneReduce:
@@ -285,58 +273,22 @@
         return value + self.full2[0].astype(F32) + self.full2[1].astype(F32)
 
 
-class TokenGather:
-    def __init__(self, ref, sources, dp_send, dp_recv, z_send, z_recv, core_send, core_recv, local):
+class Ring:
+    def __init__(self, block, z_send, z_recv, core_send, core_recv):
         self.x, self.e, self.y = position()
-        self.ref, self.sources = ref, sources
-        self.dp_send, self.dp_recv = dp_send, dp_recv
+        self.block = block
         self.z_send, self.z_recv, self.core_send, self.core_recv = z_send, z_recv, core_send, core_recv
         self.other = self.e + 1 - 2 * (self.e % 2)
         self.sent = []
-        own = [
-            pltpu.make_async_copy(s.at[:, pl.ds(SLOTTED, WHOLE)], self.landing(self.x, which), local.at[which])
-            for which, s in enumerate(sources)
-        ]
-        self.own = own
-
-    def landing(self, i, which):
-        rows = pl.ds(pl.multiple_of(self.e * TOK, TOK), TOK)
-        return self.ref.at[i, rows, pl.ds(which * WHOLE, WHOLE)]
-
-    def block(self, e, half=None):
-        rows = pl.ds(pl.multiple_of((e % EXPERTS) * TOK, TOK), TOK)
-        if half is None:
-            return self.ref.at[:, rows, :]
-        return self.ref.at[pl.ds(2 * half, 2), rows, :]
 
     def copy(self, src, dst, send, recv, device):
         c = copy_to(src, dst, send, recv, device)
         c.start()
         self.sent.append(c)
 
-    def along_dp(self):
-        for c in self.own:
-            c.start()
-        for j in range(1, N_DP):
-            for which, source in enumerate(self.sources):
-                self.copy(
-                    source.at[:, pl.ds(SLOTTED, WHOLE)], self.landing(self.x, which),
-                    self.dp_send.at[which, j], self.dp_recv.at[which, j], ((self.x + j) % N_DP, self.e, self.y),
-                )
-
-    def arrived_dp(self):
-        for c in self.own:
-            c.wait()
-        for j in range(1, N_DP):
-            for which in range(2):
-                view = self.landing((self.x + N_DP - j) % N_DP, which)
-                copy_to(
-                    view, view, self.dp_send.at[which, j], self.dp_recv.at[which, j], (self.x, self.e, self.y)
-                ).wait_recv()
-
     def view(self, e, side, distance):
         away = 2 * distance
-        return self.block(e + (EXPERTS - away if side == 0 else away), side if distance == 4 else None)
+        return self.block((e + (EXPERTS - away if side == 0 else away)) % EXPERTS, side if distance == 4 else None)
 
     def onward(self, side, distance):
         e = self.e
@@ -376,23 +328,44 @@
 def kernel(
     tokens, out_grad, gates, expert_ids, w_gate, w_up, w_down,
     input_grad, gate_grad, grad_gate, grad_up, grad_down,
-    tok, cot, sx, sd, rx, rd, rows, grads, tables, whole, w_in, w_out, pre, raw, deltas, scaled, turned, turned_scaled,
+    near, table_out, table_in, rows, grads, tables, whole, w_in, w_out, pre, raw, deltas, scaled, turned, turned_scaled,
     sums, wire, made, terms, landed_x, landed_y,
     opp_a, full_a, opp2_a, full2_a, opp_b, full_b, opp2_b, full2_b, back, ready,
-    slot_send, slot_recv, x_send, x_recv, late_send, late_recv, d_send, d_recv, g_send, g_recv,
-    dp_send, dp_recv, z_send, z_recv, core_send, core_recv,
+    slot_send, slot_recv, x_send, x_recv, d_send, d_recv, g_send, g_recv,
+    dp_send, dp_recv, z_sems,
     send_a, recv_a, send_b, recv_b, t_send, t_recv, r_send, r_recv, local,
 ):
     x, e, y = position()
     columns = pl.ds(pl.multiple_of(y * PART, LANES), PART)
+    late = pl.ds(SLOTTED, WHOLE)
+
+    def token_rows(place, half=None):
+        if half is None:
+            return pl.ds(pl.multiple_of(place * TOK, TOK), TOK)
+        return pl.ds(pl.multiple_of(place * TOK + half * (TOK // 2), TOK // 2), TOK // 2)
+
+    def whole_block(place, half=None):
+        return whole.at[:, token_rows(place), :] if half is None else whole.at[pl.ds(2 * half, 2), token_rows(place), :]
+
+    def whole_landing(i, which):
+        return whole.at[i, token_rows(e), pl.ds(which * WHOLE, WHOLE)]
+
+    ring_x = Ring(lambda p, half=None: near.at[token_rows(p, half), pl.ds(0, PART)], *[z_sems.at[k] for k in range(4)])
+    ring_d = Ring(lambda p, half=None: near.at[token_rows(p, half), pl.ds(PART, PART)], *[z_sems.at[k] for k in range(4, 8)])
+    ring_w = Ring(whole_block, *[z_sems.at[k] for k in range(8, 12)])
+
     loads = [
-        pltpu.make_async_copy(tokens.at[:, columns], tok, local.at[0]),
-        pltpu.make_async_copy(out_grad.at[:, columns], cot, local.at[1]),
+        pltpu.make_async_copy(tokens.at[:, columns], ring_x.block(e), local.at[0]),
+        pltpu.make_async_copy(out_grad.at[:, columns], ring_d.block(e), local.at[1]),
         pltpu.make_async_copy(w_gate.at[0], w_in.at[pl.ds(0, FF), :], local.at[2]),
         pltpu.make_async_copy(w_up.at[0], w_in.at[pl.ds(FPAD, FF), :], local.at[3]),
         pltpu.make_async_copy(w_down.at[0], w_out.at[pl.ds(0, FF), :], local.at[4]),
     ]
-    for c in loads:
+    own_whole = [
+        pltpu.make_async_copy(s.at[:, late], whole_landing(x, which), local.at[8 + which])
+        for which, s in enumerate((tokens, out_grad))
+    ]
+    for c in loads[:2] + own_whole + loads[2:]:
         c.start()
     peers = [(x, (e + j) % EXPERTS, y) for j in range(1, EXPERTS)]
     peers += [((x + j) % N_DP, e, y) for j in range(1, N_DP)]
@@ -414,128 +387,125 @@
     widen = jnp.where(iota((TOK, LANES), 0) == iota((TOK, LANES), 1), 1.0, 0.0).astype(BF16)
     sent = []
 
+    wide = jnp.where(iota((PADDED, LANES), 1) == TOK, gate_slots, dot(table, widen))
+    table_out[...] = wide.astype(BF16).reshape(EXPERTS, PAD, LANES)
     loads[0].wait()
-    sx[:, :, :PART] = dot(table, tok[...]).astype(BF16).reshape(EXPERTS, PAD, PART)
-    wide = jnp.where(iota((PADDED, LANES), 1) == TOK, gate_slots, dot(table, widen))
-    sx[:, :, PART:] = wide.astype(BF16).reshape(EXPERTS, PAD, LANES)
+    loads[1].wait()
     pl.semaphore_wait(barrier, len(peers))
-    cuts = ((sx, rx, 0, EARLY), (sx, rx, EARLY, PART + LANES - EARLY), (sd, rd, 0, PART))
-
-    def exchange(which):
-        source, landed, start, width = cuts[which]
-        for j in range(1, EXPERTS):
-            to = (e + j) % EXPERTS
+
+    ring_x.round(0)
+    ring_d.round(0)
+    for j in range(1, EXPERTS):
+        to = (e + j) % EXPERTS
+        c = copy_to(table_out.at[to], table_in.at[e], slot_send.at[j], slot_recv.at[j], (x, to, y))
+        c.start()
+        sent.append(c)
+    for j in range(1, N_DP):
+        for which, source in enumerate((tokens, out_grad)):
             c = copy_to(
-                source.at[to, :, pl.ds(start, width)], landed.at[e, :, pl.ds(start, width)],
-                slot_send.at[which, j], slot_recv.at[which, j], (x, to, y),
+                source.at[:, late], whole_landing(x, which),
+                dp_send.at[which, j], dp_recv.at[which, j], ((x + j) % N_DP, e, y),
             )
             c.start()
             sent.append(c)
-
-    def arrive(which):
-        source, landed, start, width = cuts[which]
-        for j in range(1, EXPERTS):
-            frm = (e + EXPERTS - j) % EXPERTS
-            view = landed.at[frm, :, pl.ds(start, width)]
-            copy_to(view, view, slot_send.at[which, j], slot_recv.at[which, j], (x, e, y)).wait_recv()
-
-    token_gather = TokenGather(
-        whole, (tokens, out_grad), dp_send, dp_recv, z_send, z_recv, core_send, core_recv, local.at[pl.ds(8, 2)]
-    )
-    exchange(0)
-    token_gather.along_dp()
-    exchange(1)
-    rx[e] = sx[e]
-    loads[1].wait()
-    sd[...] = dot(table, cot[...]).astype(BF16).reshape(EXPERTS, PAD, PART)
-    exchange(2)
-    rd[e] = sd[e]
+    table_in[e] = table_out[e]
     for ref, low in ((w_in, FF), (w_in, FPAD + FF), (w_out, FF)):
         ref[pl.ds(low, FPAD - FF), :] = jnp.zeros((FPAD - FF, D), BF16)
 
-    first = PlaneGather(rows, 0, EARLY, True, x_send, x_recv)
-    late = PlaneGather(rows, EARLY, PART - EARLY, True, late_send, late_recv)
-    second = PlaneGather(grads, 0, PART, False, d_send, d_recv)
-    steps_0, steps_1, steps_2 = first.steps(), late.steps(), second.steps()
+    gather_x = PlaneGather(rows, 0, PART, True, x_send, x_recv)
+    gather_d = PlaneGather(grads, 0, PART, False, d_send, d_recv)
+    steps_x, steps_d = gather_x.steps(), gather_d.steps()
+
+    def pick(g):
+        repeat = jnp.where(iota((LANES, EXPERTS * TOK), 0) == (iota((LANES, EXPERTS * TOK), 1) & 31), 1.0, 0.0)
+        within = jnp.where(iota((EXPERTS, EXPERTS * TOK), 0) == (iota((EXPERTS, EXPERTS * TOK), 1) >> 5), 1.0, 0.0)
+        return (dot(tables[g], repeat.astype(BF16)) * dot(block_of_row(), within.astype(BF16))).astype(BF16)
+
+    def run(*which):
+        for k in which:
+            steps_x[k]()
+            steps_d[k]()
+
+    ring_x.round(1)
+    ring_d.round(1)
     compact = compact_matrix(ROWS)
-
-    def pack(landed, ref, start, width):
-        value = dot(compact, landed[:, :, start : start + width].reshape(PADDED, width)).astype(BF16)
-        ref[x, :, pl.ds(pl.multiple_of(y * PART + start, LANES), width)] = value
-
-    def run(steps, *which):
-        for k in which:
-            steps[k]()
-
-    arrive(0)
-    pack(rx, rows, 0, EARLY)
-    run(steps_0, 0)
-    token_gather.arrived_dp()
-    token_gather.round(0)
-    arrive(1)
-    pack(rx, rows, EARLY, PART - EARLY)
-    run(steps_1, 0)
-    tables[x] = dot(compact, rx[:, :, PART:].reshape(PADDED, LANES)).astype(BF16)
+    for j in range(1, EXPERTS):
+        view = table_in.at[(e + EXPERTS - j) % EXPERTS]
+        copy_to(view, view, slot_send.at[j], slot_recv.at[j], (x, e, y)).wait_recv()
+    ring_x.round(2)
+    ring_d.round(2)
+    tables[x] = dot(compact, table_in[...].reshape(PADDED, LANES)).astype(BF16)
     for j in range(1, N_DP):
         c = copy_to(tables.at[x], tables.at[x], g_send.at[j], g_recv.at[j], ((x + j) % N_DP, e, y))
         c.start()
         sent.append(c)
-    run(steps_0, 1, 2)
-    arrive(2)
-    pack(rd, grads, 0, PART)
-    run(steps_2, 0)
-    run(steps_0, 3, 4)
-    run(steps_1, 1, 2)
-    token_gather.round(1)
-    run(steps_2, 1, 2)
-    run(steps_1, 3, 4)
-    run(steps_0, 5, 6, 7)
-    token_gather.round(2)
-    run(steps_2, 3, 4)
-    run(steps_1, 5, 6, 7)
-    token_gather.round(3)
-    run(steps_2, 5, 6, 7)
+    picker = pick(x)
+    ring_x.round(3)
+    ring_d.round(3)
+    ring_x.round(4)
+    ring_x.finish()
+    rows[x, :, columns] = dot(picker, near[:, :PART]).astype(BF16)
+    steps_x[0]()
+    ring_d.round(4)
+    ring_d.finish()
+    grads[x, :, columns] = dot(picker, near[:, PART:]).astype(BF16)
+    steps_d[0]()
+    for c in own_whole:
+        c.wait()
+    for j in range(1, N_DP):
+        for which in range(2):
+            view = whole_landing((x + N_DP - j) % N_DP, which)
+            copy_to(view, view, dp_send.at[which, j], dp_recv.at[which, j], (x, e, y)).wait_recv()
+    ring_w.round(0)
 
     reduce_a = PlaneReduce(
         sums, wire, 0, True, (2, 1, -1, 0), opp_a, full_a, opp2_a, full2_a, send_a, recv_a
     )
     reduce_b = PlaneReduce(
-        sums, wire, ROWS // 2, False, (0, -1, 1, 2), opp_b, full_b, opp2_b, full2_b, send_b, recv_b
+        sums, wire, ROWS // 2, False, (2, 1, -1, 0), opp_b, full_b, opp2_b, full2_b, send_b, recv_b
     )
-
-    def forward(g, k):
-        part = pl.ds(pl.multiple_of(k * CHUNK, CHUNK), CHUNK)
-        pre[g] += dot_t(rows[g, :, part], w_in[:, part])
-        raw[g] += dot_t(grads[g, :, part], w_out[:, part])
-
-    def begin(slot):
-        j = (0, 3, 1, 2)[slot]
-        g = (x + j) % N_DP
-        first.finish_first(slot)
-        late.finish_first(slot)
-        second.finish_second(slot)
-        if slot == 0:
-            for c in loads[2:]:
-                c.wait()
-        pre[g] = jnp.zeros((ROWS, 2 * FPAD), F32)
-        raw[g] = jnp.zeros((ROWS, FPAD), F32)
-
-        @pl.loop(0, SLOTTED // CHUNK)
+    group = [(x + j) % N_DP for j in (0, 3, 1, 2)]
+
+    def add_x(i, j):
+        part = pl.ds(pl.multiple_of((j % N_ETP) * PART, LANES), PART)
+        pre[i % N_DP] += dot_t(rows[i % N_DP, :, part], w_in[:, part])
+
+    def add_d(i, j):
+        part = pl.ds(pl.multiple_of((j % N_ETP) * PART, LANES), PART)
+        raw[i % N_DP] += dot_t(grads[i % N_DP, :, part], w_out[:, part])
+
+    def add_sides(move):
+        @pl.loop(0, 2)
         def _(k):
-            forward(g, k)
-
-    def complete(slot):
-        j = (0, 3, 1, 2)[slot]
-        g = (x + j) % N_DP
-        if slot > 0:
-            copy_to(tables.at[g], tables.at[g], g_send.at[4 - j], g_recv.at[4 - j], (x, e, y)).wait_recv()
-        repeat = jnp.where(iota((LANES, EXPERTS * TOK), 0) == (iota((LANES, EXPERTS * TOK), 1) & 31), 1.0, 0.0)
-        within = jnp.where(iota((EXPERTS, EXPERTS * TOK), 0) == (iota((EXPERTS, EXPERTS * TOK), 1) >> 5), 1.0, 0.0)
-        pick = dot(tables[g], repeat.astype(BF16)) * dot(block_of_row(), within.astype(BF16))
-        picked = dot(pick.astype(BF16), whole[g]).astype(BF16)
-        rows[g, :, SLOTTED:] = picked[:, :WHOLE]
-        grads[g, :, SLOTTED:] = picked[:, WHOLE:]
-        forward(g, SLOTTED // CHUNK)
+            add_x(x + N_DP + move, y + 3 + 2 * k)
+            add_d(x + 3 + 2 * k, y + N_ETP + move)
+
+    def add_far(slots):
+        for slot in slots:
+            gather_x.finish_far(slot)
+            gather_d.finish_far(slot)
+        start, step = {0: (0, 3), 2: (1, 1)}[slots[0]]
+
+        @pl.loop(0, 2)
+        def _(k):
+            add_x(x + start + step * k, y + 2)
+            add_d(x + 2, y + start + step * k)
+
+    def add_tokens():
+        for j in range(1, N_DP):
+            g = (x + N_DP - j) % N_DP
+            copy_to(tables.at[g], tables.at[g], g_send.at[j], g_recv.at[j], (x, e, y)).wait_recv()
+
+        @pl.loop(0, N_DP)
+        def _(g):
+            picked = dot(pick(g), whole[g]).astype(BF16)
+            rows[g, :, SLOTTED:] = picked[:, :WHOLE]
+            grads[g, :, SLOTTED:] = picked[:, WHOLE:]
+            pre[g] += dot_t(picked[:, :WHOLE], w_in[:, SLOTTED:])
+            raw[g] += dot_t(picked[:, WHOLE:], w_out[:, SLOTTED:])
+
+    def backward(slot):
+        g = group[slot]
         a, u, r = pre[g, :, :FPAD], pre[g, :, FPAD:], raw[g]
         which = slot_of_row()
         scale = tables[g, :, TOK : TOK + 1].astype(F32)
@@ -570,36 +540,63 @@
         c.start()
         loads.append(c)
 
-    begin(0)
-    token_gather.round(4)
-    begin(1)
-    token_gather.finish()
-    complete(0)
-    reduce_b.opposite(0)
-    complete(1)
-    reduce_b.opposite(1)
-    reduce_b.near(0)
-    begin(2)
-    complete(2)
-    reduce_b.opposite(2)
-    reduce_b.near(1)
-    begin(3)
-    complete(3)
+    pre[...] = jnp.zeros_like(pre)
+    raw[...] = jnp.zeros_like(raw)
+    for c in loads[2:]:
+        c.wait()
+    add_x(x, y)
+    add_d(x, y)
+    run(1, 2)
+    ring_w.round(1)
+
+    @pl.loop(0, 2)
+    def _(k):
+        add_x(x + 3 + 2 * k, y)
+        add_d(x, y + 3 + 2 * k)
+
+    run(3)
+    add_sides(0)
+    run(4)
+    ring_w.round(2)
+    add_x(x + 2, y)
+    add_d(x, y + 2)
+    run(5)
+    ring_w.round(3)
+    add_sides(-1)
+    run(6)
+    ring_w.round(4)
+    add_sides(1)
+    run(7)
+    gather_x.finish_near()
+    gather_d.finish_near()
+    add_sides(2)
+    ring_w.finish()
+    add_tokens()
+    add_far((0, 1))
+    add_far((2, 3))
+
+    backward(3)
     for k in range(4):
         reduce_a.opposite(k)
+    reduce_b.opposite(0)
+    backward(2)
+    reduce_b.opposite(1)
+    backward(1)
+    reduce_b.opposite(2)
+    reduce_a.near(0)
+    reduce_b.near(0)
+    backward(0)
     reduce_b.opposite(3)
-    reduce_b.near(2)
     for j in range(1, N_DP):
         to = (x + j) % N_DP
         c = copy_to(terms.at[to], landed_x.at[j], t_send.at[j], t_recv.at[j], (to, e, y))
         c.start()
         sent.append(c)
+    for k in range(1, 4):
+        reduce_a.near(k)
+        reduce_b.near(k)
     turned[...] = deltas[...].T
     turned_scaled[...] = scaled[...].T
-    reduce_a.near(0)
-    reduce_b.near(3)
-    for k in range(1, 4):
-        reduce_a.near(k)
     weight_grad(0)
     total = terms[x]
     for j in range(1, N_DP):
@@ -646,8 +643,35 @@
     gate_grad[...] = sum(dot(part, take) for part in parts(pairs))
     for c in loads[5:]:
         c.wait()
-    for c in sent + first.sent + late.sent + second.sent + token_gather.sent + reduce_a.sent + reduce_b.sent:
+    for c in sent + gather_x.sent + gather_d.sent + reduce_a.sent + reduce_b.sent:
         c.wait_send()
+    for ring in (ring_x, ring_d, ring_w):
+        for c in ring.sent:
+            c.wait_send()
+
+
+def copy_out(*refs):
+    count = (len(refs) - 2) // 3
+    sources, targets, held = refs[:count], refs[count : 2 * count], refs[2 * count : 3 * count]
+    into, out = refs[3 * count :]
+    steps = []
+    for source, target, place in zip(sources, targets, held):
+        if len(source.shape) < 3:
+            steps.append((source, place, target))
+            continue
+        for low, size in ((0, 176), (176, 160)):
+            view = (0, pl.ds(low, size), slice(None))
+            steps.append((source.at[view], place.at[view], target.at[view]))
+    steps = steps[::-1]
+    first = [pltpu.make_async_copy(source, place, into.at[k]) for k, (source, place, _) in enumerate(steps)]
+    second = [pltpu.make_async_copy(place, target, out.at[k]) for k, (_, place, target) in enumerate(steps)]
+    for c in first:
+        c.start()
+    for one, two in zip(first, second):
+        one.wait()
+        two.start()
+    for c in second:
+        c.wait()
 
 
 def per_device(tokens, out_grad, gates, expert_ids, w_gate, w_up, w_down):
@@ -664,7 +688,7 @@
     ]
     all_rows = N_DP * ROWS
     weight = jax.ShapeDtypeStruct(w_gate.shape, BF16)
-    input_grad, gate_grad, *weight_grads = pl.pallas_call(
+    results = pl.pallas_call(
         kernel,
         out_shape=(
             jax.ShapeDtypeStruct((count, COLS), BF16),
@@ -676,12 +700,9 @@
         in_specs=[hbm, hbm, vmem, vmem, hbm, hbm, hbm],
         out_specs=(vmem, vmem, hbm, hbm, hbm),
         scratch_shapes=[
-            pltpu.VMEM((count, PART), BF16),
-            pltpu.VMEM((count, PART), BF16),
-            pltpu.VMEM((EXPERTS, PAD, PART + LANES), BF16),
-            pltpu.VMEM((EXPERTS, PAD, PART), BF16),
-            pltpu.VMEM((EXPERTS, PAD, PART + LANES), BF16),
-            pltpu.VMEM((EXPERTS, PAD, PART), BF16),
+            pltpu.VMEM((EXPERTS * TOK, 2 * PART), BF16),
+            pltpu.VMEM((EXPERTS, PAD, LANES), BF16),
+            pltpu.VMEM((EXPERTS, PAD, LANES), BF16),
             pltpu.VMEM((N_DP, ROWS, D), BF16),
             pltpu.VMEM((N_DP, ROWS, D), BF16),
             pltpu.VMEM((N_DP, ROWS, LANES), BF16),
@@ -704,13 +725,13 @@
             *landing,
             pltpu.VMEM((EXPERTS, PAD, COLS), BF16),
             pltpu.VMEM((EXPERTS, PAD, COLS), BF16),
-            dma((3, EXPERTS)),
-            dma((3, EXPERTS)),
-            *[dma((PlaneGather.COUNT,))] * 6,
+            dma((EXPERTS,)),
+            dma((EXPERTS,)),
+            *[dma((PlaneGather.COUNT,))] * 4,
             dma((N_DP,)),
             dma((N_DP,)),
             *[dma((2, N_DP))] * 2,
-            *[dma((2, 5))] * 4,
+            dma((12, 2, 5)),
             *[dma((PlaneReduce.COUNT,))] * 4,
             dma((8,)),
             dma((8,)),
@@ -721,6 +742,15 @@
         compiler_params=pltpu.CompilerParams(collective_id=0, has_side_effects=True, vmem_limit_bytes=58 << 20),
         name="backward",
     )(tokens, out_grad, gates.T, expert_ids.T, w_gate, w_up, w_down)
+    input_grad, gate_grad, *weight_grads = pl.pallas_call(
+        copy_out,
+        out_shape=tuple(jax.ShapeDtypeStruct(r.shape, r.dtype) for r in results),
+        in_specs=[hbm] * 5,
+        out_specs=(hbm,) * 5,
+        scratch_shapes=[*[pltpu.VMEM(r.shape, r.dtype) for r in results], dma((8,)), dma((8,))],
+        compiler_params=pltpu.CompilerParams(vmem_limit_bytes=58 << 20),
+        name="outputs",
+    )(*results)
     return input_grad, gate_grad.T, *weight_grads
 
 

time: 137 us -> 125 us (0.912)
  local copies, waits for them, and re-layouts: 9.47 us -> 0 us
  Pallas kernels: 127 us -> 123 us
    unnamed x9 -> x0, local copies, waits for them, and re-layouts: 9.47 us -> none
    pallas_call x1, Pallas kernels: 127 us -> 118 us  [per_device(): pl.pallas_call(kernel, out_shape=(jax.ShapeDtypeStruct((count, COLS), BF1...]
    pallas_call x0 -> x1, Pallas kernels: none -> 5.46 us  [per_device(): pl.pallas_call(copy_out, out_shape=tuple((jax.ShapeDtypeStruct(r.shape, r...]
where the time goes in v4:
time: 125 us; the launch traced here: 124 us
  Pallas kernels  123 us (98%)
    pallas_call x1, Pallas kernels, per_device(): pl.pallas_call(kernel, out_shape=(jax.ShapeDtypeStruct((count, COLS), BF1...  118 us
    pallas_call x1, Pallas kernels, per_device(): pl.pallas_call(copy_out, out_shape=tuple((jax.ShapeDtypeStruct(r.shape, r...  5.46 us

profile of v4, /device:TPU:1, one launch (start us, length us, event | category | flops | bytes accessed | tf_op | source)
XLA Modules:
  0.0 124.2 jit_solution(5466073132607875336)
XLA Ops:
  0.6 117.9 %backward.1 = (bf16[32,768]{1,0:T(8,128)(2,1)}, f32[4,8]{1,0:T(4,128)}, bf16[1,336,3072]{2,1,0:T(8,128)(2,1)}, bf16[1,336,3072]{2,1,0:T(8,128)(2,1)}, bf16[1,336,3072]{2,1,0:T(8,128)(2,1)}) custom-call(bf16[32,3072]{1,0:T(8,128)(2,1)} %tokens.1, bf16[32,3072]{1,0:T(8,128)(2,1)} %out_grad.1, bf16[4,32]{1,0:T(4,128)(2,1)} %bitcast.4, s32[4,32]{1,0:T(4,128)} %bitcast.3, ...), custom_call_target="tpu_custom_call" | custom-call | tf_op jit(solution)/shard_map/backward/pallas_call | solution.py:691
  118.5 5.5 %outputs.1 = (bf16[32,768]{1,0:T(8,128)(2,1)}, f32[4,8]{1,0:T(4,128)}, bf16[1,336,3072]{2,1,0:T(8,128)(2,1)}, bf16[1,336,3072]{2,1,0:T(8,128)(2,1)}, bf16[1,336,3072]{2,1,0:T(8,128)(2,1)}) custom-call(bf16[32,768]{1,0:T(8,128)(2,1)} %get-tuple-element.15.refs_0_, f32[4,8]{1,0:T(4,128)} %get-tuple-element.16.refs_1_, ...), custom_call_target="tpu_custom_call" | custom-call | tf_op jit(solution)/shard_map/outputs/pallas_call | solution.py:745

commit v5 on v4

--- a/solution.py
+++ b/solution.py
@@ -36,6 +36,16 @@
     return jnp.where(((k >> 4) * CAP + (k & 15) == r) & ((k & 15) < CAP), 1.0, 0.0).astype(BF16)
 
 
+def place_of(block):
+    away = ((block >> 1) + 8 - (lax.axis_index("expert") >> 1)) & 7
+    return jnp.where(away > 4, 2 * (8 - away), jnp.maximum(2 * away - 1, 0)) * 2 + (block & 1)
+
+
+def placed_matrix():
+    r, k = iota((ROWS, PADDED), 0), iota((ROWS, PADDED), 1)
+    return jnp.where((place_of(k >> 4) * CAP + (k & 15) == r) & ((k & 15) < CAP), 1.0, 0.0).astype(BF16)
+
+
 def same_row(which):
     k, m = iota((PADDED, PADDED), 0), iota((PADDED, PADDED), 1)
     return jnp.where(m == (k >> 4) * PAD + CAP + which, 1.0, 0.0).astype(BF16)
@@ -51,8 +61,10 @@
     return jnp.where((k & 15) == c, 1.0, 0.0).astype(BF16)
 
 
-def block_of_row():
+def block_of_row(placed=True):
     r, b = iota((ROWS, EXPERTS), 0), iota((ROWS, EXPERTS), 1)
+    if not placed:
+        b = place_of(b)
     return jnp.where((r >= b * CAP) & (r < b * CAP + CAP), 1.0, 0.0).astype(BF16)
 
 
@@ -96,7 +108,7 @@
 
 
 class PlaneGather:
-    COUNT = 22
+    COUNT = 26
 
     def __init__(self, ref, start, width, dp_first, send_sems, recv_sems):
         x, e, y = position()
@@ -130,6 +142,23 @@
     def wait(self, view, index):
         self.copy(view, index, self.device(self.a, self.b)).wait_recv()
 
+    def own(self, half):
+        a, b = self.a, self.b
+        view = self.at(a, b, half)
+        self.send(view, 22 * half, self.device(a + 1, b))
+        self.send(view, 1 + 22 * half, self.device(a - 1, b))
+        self.send(view, 4 + 20 * half, self.device(a, b + 1))
+        self.send(view, 5 + 20 * half, self.device(a, b - 1))
+
+    def forward_own(self):
+        a, b = self.a, self.b
+        self.wait(self.at(a, b - 1, 0), 4)
+        self.send(self.at(a, b - 1, 0), 14, self.device(a, b + 1))
+        self.wait(self.at(a, b + 1, 1), 25)
+        self.send(self.at(a, b + 1, 1), 15, self.device(a, b - 1))
+        self.wait(self.at(a, b - 1, 1), 24)
+        self.wait(self.at(a, b + 1, 0), 5)
+
     def both_second(self, i, slot, half=None):
         view = self.at(i, self.b, half)
         self.send(view, 4 + 2 * slot, self.device(self.a, self.b + 1))
@@ -144,19 +173,16 @@
     def steps(self):
         a, b = self.a, self.b
 
-        def own():
-            self.send(self.at(a, b), 0, self.device(a + 1, b))
-            self.send(self.at(a, b), 1, self.device(a - 1, b))
-            self.both_second(a, 0)
-
         def lower():
-            self.wait(self.at(a - 1, b), 0)
+            self.wait(self.at(a - 1, b, 0), 0)
             self.send(self.at(a - 1, b, 0), 2, self.device(a + 1, b))
+            self.wait(self.at(a - 1, b, 1), 22)
             self.both_second(a - 1, 1)
 
         def upper():
-            self.wait(self.at(a + 1, b), 1)
+            self.wait(self.at(a + 1, b, 1), 23)
             self.send(self.at(a + 1, b, 1), 3, self.device(a - 1, b))
+            self.wait(self.at(a + 1, b, 0), 1)
             self.both_second(a + 1, 2)
 
         def opposite():
@@ -172,10 +198,10 @@
             self.send(self.at(a + 2, b + 1, 1), 21, self.device(a, b - 1))
 
         return [
-            own,
+            None,
             lower,
             upper,
-            lambda: self.forward_second(a, 0),
+            self.forward_own,
             opposite,
             lambda: self.forward_second(a - 1, 1),
             lambda: self.forward_second(a + 1, 2),
@@ -314,15 +340,16 @@
         for side in range(2):
             self.onward(side, distance)
 
-    def finish(self):
-        for distance in range(5):
-            for side in range(2):
-                if distance > 0 or side == 0:
-                    view = self.view(self.other, side, distance)
-                    copy_to(
-                        view, view, self.core_send.at[side, distance], self.core_recv.at[side, distance],
-                        (self.x, self.e, self.y),
-                    ).wait_recv()
+    NEAR = ((0, 0), (0, 1), (1, 1), (1, 2))
+    FAR = ((0, 2), (0, 3), (1, 3), (0, 4), (1, 4))
+
+    def finish(self, which):
+        for side, distance in which:
+            view = self.view(self.other, side, distance)
+            copy_to(
+                view, view, self.core_send.at[side, distance], self.core_recv.at[side, distance],
+                (self.x, self.e, self.y),
+            ).wait_recv()
 
 
 def kernel(
@@ -419,37 +446,55 @@
     def pick(g):
         repeat = jnp.where(iota((LANES, EXPERTS * TOK), 0) == (iota((LANES, EXPERTS * TOK), 1) & 31), 1.0, 0.0)
         within = jnp.where(iota((EXPERTS, EXPERTS * TOK), 0) == (iota((EXPERTS, EXPERTS * TOK), 1) >> 5), 1.0, 0.0)
-        return (dot(tables[g], repeat.astype(BF16)) * dot(block_of_row(), within.astype(BF16))).astype(BF16)
+        return (dot(tables[g], repeat.astype(BF16)) * dot(block_of_row(False), within.astype(BF16))).astype(BF16)
 
     def run(*which):
         for k in which:
             steps_x[k]()
             steps_d[k]()
 
-    ring_x.round(1)
-    ring_d.round(1)
-    compact = compact_matrix(ROWS)
+    half = ROWS // 2
+
+    def own_half(ref, start, h):
+        r, m = iota((half, EXPERTS // 2 * TOK), 0), iota((half, EXPERTS // 2 * TOK), 1)
+        within = (r >= (m >> 5) * CAP) & (r < (m >> 5) * CAP + CAP)
+        lane, m = iota((LANES, EXPERTS // 2 * TOK), 0), iota((LANES, EXPERTS // 2 * TOK), 1)
+        repeat = jnp.where(lane == (m & 31), 1.0, 0.0).astype(BF16)
+        own = pl.ds(h * half, half)
+        picker = jnp.where(within, dot(tables[x, own, :], repeat), 0.0).astype(BF16)
+        taken = []
+        for away in ((0, 1, 7, 2), (6, 3, 5, 4))[h]:
+            low = pl.multiple_of((((e // 2) + away) % 8) * (2 * TOK), 2 * TOK)
+            taken.append(near[pl.ds(low, 2 * TOK), start : start + PART])
+        ref[x, own, columns] = dot(picker, jnp.concatenate(taken, axis=0)).astype(BF16)
+
+    for k in range(1, 3):
+        ring_x.round(k)
+        ring_d.round(k)
     for j in range(1, EXPERTS):
         view = table_in.at[(e + EXPERTS - j) % EXPERTS]
         copy_to(view, view, slot_send.at[j], slot_recv.at[j], (x, e, y)).wait_recv()
-    ring_x.round(2)
-    ring_d.round(2)
-    tables[x] = dot(compact, table_in[...].reshape(PADDED, LANES)).astype(BF16)
+    tables[x] = dot(placed_matrix(), table_in[...].reshape(PADDED, LANES)).astype(BF16)
     for j in range(1, N_DP):
         c = copy_to(tables.at[x], tables.at[x], g_send.at[j], g_recv.at[j], ((x + j) % N_DP, e, y))
         c.start()
         sent.append(c)
-    picker = pick(x)
+    ring_x.finish(Ring.NEAR)
+    own_half(rows, 0, 0)
+    gather_x.own(0)
     ring_x.round(3)
     ring_d.round(3)
+    ring_d.finish(Ring.NEAR)
+    own_half(grads, PART, 0)
+    gather_d.own(0)
     ring_x.round(4)
-    ring_x.finish()
-    rows[x, :, columns] = dot(picker, near[:, :PART]).astype(BF16)
-    steps_x[0]()
     ring_d.round(4)
-    ring_d.finish()
-    grads[x, :, columns] = dot(picker, near[:, PART:]).astype(BF16)
-    steps_d[0]()
+    ring_x.finish(Ring.FAR)
+    own_half(rows, 0, 1)
+    gather_x.own(1)
+    ring_d.finish(Ring.FAR)
+    own_half(grads, PART, 1)
+    gather_d.own(1)
     for c in own_whole:
         c.wait()
     for j in range(1, N_DP):
@@ -570,7 +615,7 @@
     gather_x.finish_near()
     gather_d.finish_near()
     add_sides(2)
-    ring_w.finish()
+    ring_w.finish(Ring.NEAR + Ring.FAR)
     add_tokens()
     add_far((0, 1))
     add_far((2, 3))
@@ -609,28 +654,43 @@
         sent.append(c)
     reduce_a.second_opposite()
     reduce_b.second_opposite()
-    weight_grad(1)
     for side in range(2):
         reduce_a.second_near(side)
         reduce_b.second_near(side)
-    weight_grad(2)
     for j in range(1, N_ETP):
         copy_to(landed_y.at[j], landed_y.at[j], t_send.at[3 + j], t_recv.at[3 + j], (x, e, y)).wait_recv()
         total = total + landed_y[j]
     spare = sum(t_dot(extra_row(which), part) for which, part in enumerate(parts(total)))
-    summed = jnp.concatenate([reduce_a.finish(), reduce_b.finish()], axis=0).astype(BF16)
-    padded = t_dot(compact, summed)
-    ready[:, :, :LANES] = (padded[:, :LANES] + spare).astype(BF16).reshape(EXPERTS, PAD, LANES)
-    ready[:, :, LANES:] = padded[:, LANES:].astype(BF16).reshape(EXPERTS, PAD, COLS - LANES)
-    for j in range(1, EXPERTS):
-        to = (e + j) % EXPERTS
-        c = copy_to(ready.at[to], back.at[e], r_send.at[j], r_recv.at[j], (x, to, y))
-        c.start()
-        sent.append(c)
-    back[e] = ready[e]
-    for j in range(1, EXPERTS):
-        frm = (e + EXPERTS - j) % EXPERTS
-        copy_to(back.at[frm], back.at[frm], r_send.at[j], r_recv.at[j], (x, e, y)).wait_recv()
+    r, k = iota((half, PADDED // 2), 0), iota((half, PADDED // 2), 1)
+    spread = jnp.where(((k >> 4) * CAP + (k & 15) == r) & ((k & 15) < CAP), 1.0, 0.0).astype(BF16)
+    core = e % 2
+    for h, reduce in ((1, reduce_b), (0, reduce_a)):
+        padded = t_dot(spread, reduce.finish().astype(BF16))
+        own = pl.ds(h * (EXPERTS // 2), EXPERTS // 2)
+        extra = spare[h * (PADDED // 2) : (h + 1) * (PADDED // 2)]
+        ready[own, :, :LANES] = (padded[:, :LANES] + extra).astype(BF16).reshape(EXPERTS // 2, PAD, LANES)
+        ready[own, :, LANES:] = padded[:, LANES:].astype(BF16).reshape(EXPERTS // 2, PAD, COLS - LANES)
+        for k in range(3, -1, -1):
+            away = ((0, 1, 7, 2), (6, 3, 5, 4))[h][k]
+            for flip in range(2):
+                to_core = core if flip == 0 else 1 - core
+                source = ready.at[8 * h + 2 * k + to_core]
+                if away == 0 and flip == 0:
+                    back[e] = source[...]
+                    continue
+                to = ((e // 2 + away) % 8) * 2 + to_core
+                c = copy_to(source, back.at[e], r_send.at[away, flip], r_recv.at[away, flip], (x, to, y))
+                c.start()
+                sent.append(c)
+    weight_grad(1)
+    weight_grad(2)
+    for away in range(8):
+        for flip in range(2):
+            if away > 0 or flip > 0:
+                frm = ((e // 2 + 8 - away) % 8) * 2 + (core if flip == 0 else 1 - core)
+                copy_to(
+                    back.at[frm], back.at[frm], r_send.at[away, flip], r_recv.at[away, flip], (x, e, y)
+                ).wait_recv()
     block = back[...].reshape(PADDED, COLS)
     input_grad[...] = t_dot(table, block).astype(BF16)
     lanes = block[:, :LANES]
@@ -735,8 +795,8 @@
             *[dma((PlaneReduce.COUNT,))] * 4,
             dma((8,)),
             dma((8,)),
-            dma((EXPERTS,)),
-            dma((EXPERTS,)),
+            dma((8, 2)),
+            dma((8, 2)),
             dma((10,)),
         ],
         compiler_params=pltpu.CompilerParams(collective_id=0, has_side_effects=True, vmem_limit_bytes=58 << 20),

time: 125 us -> 118 us (0.944)
  Pallas kernels: 123 us -> 117 us
    pallas_call x1, Pallas kernels: 118 us -> 111 us  [per_device(): pl.pallas_call(kernel, out_shape=(jax.ShapeDtypeStruct((count, COLS), BF1...]
where the time goes in v5:
time: 118 us
  Pallas kernels  117 us (99%)
    pallas_call x1, Pallas kernels, per_device(): pl.pallas_call(kernel, out_shape=(jax.ShapeDtypeStruct((count, COLS), BF1...  111 us
    pallas_call x1, Pallas kernels, per_device(): pl.pallas_call(copy_out, out_shape=tuple((jax.ShapeDtypeStruct(r.shape, r...  5.46 us

profile of v5, /device:TPU:1, one launch (start us, length us, event | category | flops | bytes accessed | tf_op | source)
XLA Modules:
  0.0 117.5 jit_solution(14417478914442176861)
XLA Ops:
  0.6 111.3 %backward.1 = (bf16[32,768]{1,0:T(8,128)(2,1)}, f32[4,8]{1,0:T(4,128)}, bf16[1,336,3072]{2,1,0:T(8,128)(2,1)}, bf16[1,336,3072]{2,1,0:T(8,128)(2,1)}, bf16[1,336,3072]{2,1,0:T(8,128)(2,1)}) custom-call(bf16[32,3072]{1,0:T(8,128)(2,1)} %tokens.1, bf16[32,3072]{1,0:T(8,128)(2,1)} %out_grad.1, bf16[4,32]{1,0:T(4,128)(2,1)} %bitcast.4, s32[4,32]{1,0:T(4,128)} %bitcast.3, ...), custom_call_target="tpu_custom_call" | custom-call | tf_op jit(solution)/shard_map/backward/pallas_call | solution.py:751
  111.9 5.5 %outputs.1 = (bf16[32,768]{1,0:T(8,128)(2,1)}, f32[4,8]{1,0:T(4,128)}, bf16[1,336,3072]{2,1,0:T(8,128)(2,1)}, bf16[1,336,3072]{2,1,0:T(8,128)(2,1)}, bf16[1,336,3072]{2,1,0:T(8,128)(2,1)}) custom-call(bf16[32,768]{1,0:T(8,128)(2,1)} %get-tuple-element.15.refs_0_, f32[4,8]{1,0:T(4,128)} %get-tuple-element.16.refs_1_, ...), custom_call_target="tpu_custom_call" | custom-call | tf_op jit(solution)/shard_map/outputs/pallas_call | solution.py:805

commit v6 on v5

--- a/solution.py
+++ b/solution.py
@@ -257,10 +257,11 @@
         self.send(self.at(a + 2, j, 0, q), self.opp.at[0, k], 4 * k, self.device(a + 1, b))
         self.send(self.at(a + 2, j, q, q), self.opp.at[1, k], 4 * k + 1, self.device(a - 1, b))
 
-    def near(self, k):
+    def near(self, k, sides=(0, 1)):
         a, b, q, h = self.a, self.b, self.QUARTER, self.HALF
         j = b + self.order[k]
-        for side, to in ((0, a + 1), (1, a - 1)):
+        for side in sides:
+            to = a + 1 if side == 0 else a - 1
             self.wait(self.opp.at[side, k], 4 * k + side)
             own = self.at(to, j, side * q, q, self.ref)[...]
             self.at(to, j, side * q, q)[...] = (own + self.opp[side, k].astype(F32)).astype(BF16)
@@ -363,6 +364,12 @@
     send_a, recv_a, send_b, recv_b, t_send, t_recv, r_send, r_recv, local,
 ):
     x, e, y = position()
+    peers = [(x, (e + j) % EXPERTS, y) for j in range(1, EXPERTS)]
+    peers += [((x + j) % N_DP, e, y) for j in range(1, N_DP)]
+    peers += [(x, e, (y + j) % N_ETP) for j in range(1, N_ETP)]
+    barrier = pltpu.get_barrier_semaphore()
+    for device in peers:
+        pl.semaphore_signal(barrier, inc=1, device_id=device, device_id_type=MESH)
     columns = pl.ds(pl.multiple_of(y * PART, LANES), PART)
     late = pl.ds(SLOTTED, WHOLE)
 
@@ -394,13 +401,6 @@
     ]
     for c in loads[:2] + own_whole + loads[2:]:
         c.start()
-    peers = [(x, (e + j) % EXPERTS, y) for j in range(1, EXPERTS)]
-    peers += [((x + j) % N_DP, e, y) for j in range(1, N_DP)]
-    peers += [(x, e, (y + j) % N_ETP) for j in range(1, N_ETP)]
-    barrier = pltpu.get_barrier_semaphore()
-    for device in peers:
-        pl.semaphore_signal(barrier, inc=1, device_id=device, device_id_type=MESH)
-
     expert, place = iota((PADDED, TOK), 0) >> 4, iota((PADDED, TOK), 0) & 15
     ids, weight = expert_ids[...], gates[...].astype(F32)
     chosen = [jnp.where(ids[k : k + 1, :] == expert, 1.0, 0.0) for k in range(TOP)]
@@ -536,20 +536,17 @@
             add_x(x + start + step * k, y + 2)
             add_d(x + 2, y + start + step * k)
 
-    def add_tokens():
-        for j in range(1, N_DP):
-            g = (x + N_DP - j) % N_DP
-            copy_to(tables.at[g], tables.at[g], g_send.at[j], g_recv.at[j], (x, e, y)).wait_recv()
-
-        @pl.loop(0, N_DP)
-        def _(g):
+    def add_tokens(low, high):
+        @pl.loop(low, high)
+        def _(k):
+            g = (x + k) % N_DP
             picked = dot(pick(g), whole[g]).astype(BF16)
             rows[g, :, SLOTTED:] = picked[:, :WHOLE]
             grads[g, :, SLOTTED:] = picked[:, WHOLE:]
             pre[g] += dot_t(picked[:, :WHOLE], w_in[:, SLOTTED:])
             raw[g] += dot_t(picked[:, WHOLE:], w_out[:, SLOTTED:])
 
-    def backward(slot):
+    def backward(slot, send=None):
         g = group[slot]
         a, u, r = pre[g, :, :FPAD], pre[g, :, FPAD:], raw[g]
         which = slot_of_row()
@@ -565,12 +562,18 @@
         deltas[own, :FPAD] = (hidden * u * sigmoid * (1.0 + a * (1.0 - sigmoid))).astype(BF16)
         deltas[own, FPAD:] = (hidden * activated).astype(BF16)
 
-        @pl.loop(0, N_ETP)
-        def _(k):
+        def columns_of(k):
             part = pl.ds(pl.multiple_of(k * COLS, COLS), COLS)
             value = dot(deltas[own, :], w_in[:, part])
             sums[g, :, part] = value
             wire[g, :, part] = value.astype(BF16)
+
+        if send is None:
+            pl.loop(0, N_ETP)(columns_of)
+            return
+        for k in range(N_ETP):
+            columns_of((y + N_ETP + reduce_a.order[k]) % N_ETP)
+            send(k)
 
     def weight_grad(which):
         source = (rows, rows, grads)[which]
@@ -612,37 +615,46 @@
     ring_w.round(4)
     add_sides(1)
     run(7)
+    for j in range(1, N_DP):
+        g = (x + N_DP - j) % N_DP
+        copy_to(tables.at[g], tables.at[g], g_send.at[j], g_recv.at[j], (x, e, y)).wait_recv()
     gather_x.finish_near()
     gather_d.finish_near()
     add_sides(2)
     ring_w.finish(Ring.NEAR + Ring.FAR)
-    add_tokens()
+    add_tokens(0, 4)
     add_far((0, 1))
     add_far((2, 3))
 
-    backward(3)
-    for k in range(4):
+    def send_opposite(k):
         reduce_a.opposite(k)
-    reduce_b.opposite(0)
+        if k == 0:
+            reduce_b.opposite(0)
+
+    backward(3, send_opposite)
     backward(2)
     reduce_b.opposite(1)
+    reduce_b.near(0)
+    reduce_a.near(0, (0,))
+    reduce_a.near(1, (0,))
     backward(1)
     reduce_b.opposite(2)
-    reduce_a.near(0)
-    reduce_b.near(0)
+    reduce_a.near(0, (1,))
+    reduce_a.near(1, (1,))
+    reduce_b.near(1)
+    reduce_a.near(2)
     backward(0)
     reduce_b.opposite(3)
+    reduce_b.near(2)
     for j in range(1, N_DP):
         to = (x + j) % N_DP
         c = copy_to(terms.at[to], landed_x.at[j], t_send.at[j], t_recv.at[j], (to, e, y))
         c.start()
         sent.append(c)
-    for k in range(1, 4):
-        reduce_a.near(k)
-        reduce_b.near(k)
     turned[...] = deltas[...].T
     turned_scaled[...] = scaled[...].T
-    weight_grad(0)
+    reduce_a.second_opposite()
+    reduce_b.second_opposite()
     total = terms[x]
     for j in range(1, N_DP):
         copy_to(landed_x.at[j], landed_x.at[j], t_send.at[j], t_recv.at[j], (x, e, y)).wait_recv()
@@ -652,11 +664,13 @@
         c = copy_to(landed_y.at[0], landed_y.at[j], t_send.at[3 + j], t_recv.at[3 + j], (x, e, (y + j) % N_ETP))
         c.start()
         sent.append(c)
-    reduce_a.second_opposite()
-    reduce_b.second_opposite()
-    for side in range(2):
-        reduce_a.second_near(side)
-        reduce_b.second_near(side)
+    reduce_a.second_near(0)
+    reduce_b.second_near(0)
+    reduce_a.near(3)
+    reduce_b.near(3)
+    weight_grad(0)
+    reduce_a.second_near(1)
+    reduce_b.second_near(1)
     for j in range(1, N_ETP):
         copy_to(landed_y.at[j], landed_y.at[j], t_send.at[3 + j], t_recv.at[3 + j], (x, e, y)).wait_recv()
         total = total + landed_y[j]

time: 118 us -> 116 us (0.983)
  Pallas kernels: 117 us -> 115 us
    pallas_call x1, Pallas kernels: 111 us -> 110 us  [per_device(): pl.pallas_call(kernel, out_shape=(jax.ShapeDtypeStruct((count, COLS), BF1...]
where the time goes in v6:
time: 116 us
  Pallas kernels  115 us (99%)
    pallas_call x1, Pallas kernels, per_device(): pl.pallas_call(kernel, out_shape=(jax.ShapeDtypeStruct((count, COLS), BF1...  110 us
    pallas_call x1, Pallas kernels, per_device(): pl.pallas_call(copy_out, out_shape=tuple((jax.ShapeDtypeStruct(r.shape, r...  5.46 us

profile of v6, /device:TPU:1, one launch (start us, length us, event | category | flops | bytes accessed | tf_op | source)
XLA Modules:
  0.0 116.1 jit_solution(17379325820165219407)
XLA Ops:
  0.6 109.8 %backward.1 = (bf16[32,768]{1,0:T(8,128)(2,1)}, f32[4,8]{1,0:T(4,128)}, bf16[1,336,3072]{2,1,0:T(8,128)(2,1)}, bf16[1,336,3072]{2,1,0:T(8,128)(2,1)}, bf16[1,336,3072]{2,1,0:T(8,128)(2,1)}) custom-call(bf16[32,3072]{1,0:T(8,128)(2,1)} %tokens.1, bf16[32,3072]{1,0:T(8,128)(2,1)} %out_grad.1, bf16[4,32]{1,0:T(4,128)(2,1)} %bitcast.4, s32[4,32]{1,0:T(4,128)} %bitcast.3, ...), custom_call_target="tpu_custom_call" | custom-call | tf_op jit(solution)/shard_map/backward/pallas_call | solution.py:765
  110.4 5.5 %outputs.1 = (bf16[32,768]{1,0:T(8,128)(2,1)}, f32[4,8]{1,0:T(4,128)}, bf16[1,336,3072]{2,1,0:T(8,128)(2,1)}, bf16[1,336,3072]{2,1,0:T(8,128)(2,1)}, bf16[1,336,3072]{2,1,0:T(8,128)(2,1)}) custom-call(bf16[32,768]{1,0:T(8,128)(2,1)} %get-tuple-element.15.refs_0_, f32[4,8]{1,0:T(4,128)} %get-tuple-element.16.refs_1_, ...), custom_call_target="tpu_custom_call" | custom-call | tf_op jit(solution)/shard_map/outputs/pallas_call | solution.py:819

commit v7 on v6

--- a/solution.py
+++ b/solution.py
@@ -525,16 +525,12 @@
             add_x(x + N_DP + move, y + 3 + 2 * k)
             add_d(x + 3 + 2 * k, y + N_ETP + move)
 
-    def add_far(slots):
-        for slot in slots:
-            gather_x.finish_far(slot)
-            gather_d.finish_far(slot)
-        start, step = {0: (0, 3), 2: (1, 1)}[slots[0]]
-
-        @pl.loop(0, 2)
-        def _(k):
-            add_x(x + start + step * k, y + 2)
-            add_d(x + 2, y + start + step * k)
+    def add_far(slot):
+        gather_x.finish_far(slot)
+        gather_d.finish_far(slot)
+        move = (0, 3, 1, 2)[slot]
+        add_x(x + move, y + 2)
+        add_d(x + 2, y + move)
 
     def add_tokens(low, high):
         @pl.loop(low, high)
@@ -623,8 +619,8 @@
     add_sides(2)
     ring_w.finish(Ring.NEAR + Ring.FAR)
     add_tokens(0, 4)
-    add_far((0, 1))
-    add_far((2, 3))
+    for slot in range(4):
+        add_far(slot)
 
     def send_opposite(k):
         reduce_a.opposite(k)
@@ -733,7 +729,7 @@
         if len(source.shape) < 3:
             steps.append((source, place, target))
             continue
-        for low, size in ((0, 176), (176, 160)):
+        for low, size in ((0, 96), (96, 80), (176, 80), (256, 80)):
             view = (0, pl.ds(low, size), slice(None))
             steps.append((source.at[view], place.at[view], target.at[view]))
     steps = steps[::-1]
@@ -821,7 +817,7 @@
         out_shape=tuple(jax.ShapeDtypeStruct(r.shape, r.dtype) for r in results),
         in_specs=[hbm] * 5,
         out_specs=(hbm,) * 5,
-        scratch_shapes=[*[pltpu.VMEM(r.shape, r.dtype) for r in results], dma((8,)), dma((8,))],
+        scratch_shapes=[*[pltpu.VMEM(r.shape, r.dtype) for r in results], dma((16,)), dma((16,))],
         compiler_params=pltpu.CompilerParams(vmem_limit_bytes=58 << 20),
         name="outputs",
     )(*results)

time: 116 us -> 116 us (level)
  no operation moved by 1% of the time
where the time goes in v7:
time: 116 us
  Pallas kernels  115 us (99%)
    pallas_call x1, Pallas kernels, per_device(): pl.pallas_call(kernel, out_shape=(jax.ShapeDtypeStruct((count, COLS), BF1...  110 us
    pallas_call x1, Pallas kernels, per_device(): pl.pallas_call(copy_out, out_shape=tuple((jax.ShapeDtypeStruct(r.shape, r...  5.52 us

profile of v7, /device:TPU:1, one launch (start us, length us, event | category | flops | bytes accessed | tf_op | source)
XLA Modules:
  0.0 116.2 jit_solution(9556615572737291381)
XLA Ops:
  0.6 109.9 %backward.1 = (bf16[32,768]{1,0:T(8,128)(2,1)}, f32[4,8]{1,0:T(4,128)}, bf16[1,336,3072]{2,1,0:T(8,128)(2,1)}, bf16[1,336,3072]{2,1,0:T(8,128)(2,1)}, bf16[1,336,3072]{2,1,0:T(8,128)(2,1)}) custom-call(bf16[32,3072]{1,0:T(8,128)(2,1)} %tokens.1, bf16[32,3072]{1,0:T(8,128)(2,1)} %out_grad.1, bf16[4,32]{1,0:T(4,128)(2,1)} %bitcast.4, s32[4,32]{1,0:T(4,128)} %bitcast.3, ...), custom_call_target="tpu_custom_call" | custom-call | tf_op jit(solution)/shard_map/backward/pallas_call | solution.py:761
  110.5 5.5 %outputs.1 = (bf16[32,768]{1,0:T(8,128)(2,1)}, f32[4,8]{1,0:T(4,128)}, bf16[1,336,3072]{2,1,0:T(8,128)(2,1)}, bf16[1,336,3072]{2,1,0:T(8,128)(2,1)}, bf16[1,336,3072]{2,1,0:T(8,128)(2,1)}) custom-call(bf16[32,768]{1,0:T(8,128)(2,1)} %get-tuple-element.15.refs_0_, f32[4,8]{1,0:T(4,128)} %get-tuple-element.16.refs_1_, ...), custom_call_target="tpu_custom_call" | custom-call | tf_op jit(solution)/shard_map/outputs/pallas_call | solution.py:815
